TPU v7x, 32 devices: a whole 2x2x4 slice. The times are simulated.
32 devices in a mesh: doc: 4 (over x, core), term: 8 (over z, y).
Axes of the slice: x: 2, y: 2, z: 4, core: 2. Of those that a mesh axis runs over, the one named last changes fastest.
Arguments:
- query_states: bfloat16 [256, 32, 768], P('doc'), may hold values from -6 to 6
- token_ids: int32 [256, 32], P('doc'), may hold values from 0 to 30521, as said below
- transform_weight: bfloat16 [768, 768], replicated, may hold values from -0.21875 to 0.21875
- transform_bias: float32 [768], replicated, may hold values from -3 to 3
- norm_gain: float32 [768], replicated, may hold values from 0.5 to 1.5
- norm_bias: float32 [768], replicated, may hold values from -3 to 3
- decoder_weight: bfloat16 [768, 30720], P(None, 'term'), may hold values from -0.21875 to 0.21875
- decoder_bias: float32 [30720], P('term'), may hold values from -2.5 to 0.5
- candidates: int32 [256, 32], P('doc'), may hold values from 0 to 63, all different within a row; in each aligned block of 64 rows (0 to 63, 64 to 127, ...) at most 32 rows name the same one
- occupancy: int32 [64, 240], P('doc', 'term'), may hold values 0 or 1
- doc_blocks: bfloat16 [64, 240, 128, 128], P('doc', 'term'), may hold values from -0.046875 to 0.046875
Outputs:
- query_weights: bfloat16 [256, 30720], P('doc', 'term')
- scores: float32 [256, 32, 128], P('doc', None, 'term')
Inputs may be any that keep to these rules, and one draw needn't show every extreme that they name: `token_ids`: id 0 marks padding: a query has non-zero ids at its first positions, at least 8 of them, and 0 after them. `candidates`: A query names 32 different tiles; among the 64 queries of one doc index no tile is named by more than 32 of them.
All inputs are finite; a program needn't handle non-finite values. No bound on the sum of `occupancy` on one device may be relied on, other than what follows from the above.
Results may differ from a plain program's by a relative error of at most 0.0041.
Values may be sent and summed in bfloat16 or wider, within the bound.
No kernel may reach another device: no remote copies, remote signals or barrier semaphores. Data moves between devices by JAX's collectives and lax.ppermute only.
A program may use at most 128 MiB of HBM per device.

v0:
```python
import jax
import jax.numpy as jnp
from jax import lax
from jax.sharding import PartitionSpec as P

VOCAB = 30522
MOST = 32


def tile_ranks(cand_rows, tile_total):
    tile_index = lax.iota(jnp.int32, tile_total)
    tile_hits = jnp.sum((cand_rows[..., None] == tile_index).astype(jnp.int32), axis=-2)
    tile_before = jnp.cumsum(tile_hits, axis=-2) - tile_hits
    return (tile_hits, tile_before)


def slot_sources(hits_by_tile, before_by_tile, capacity):
    row_total = hits_by_tile.shape[-1]
    slot_index = lax.iota(jnp.int32, capacity)
    chosen = (hits_by_tile[..., None, :] > 0) & (
        before_by_tile[..., None, :] == slot_index[:, None]
    )
    source_row = jnp.sum(jnp.where(chosen, lax.iota(jnp.int32, row_total), 0), axis=-1)
    return (source_row, jnp.any(chosen, axis=-1))


def body(
    query_states,
    token_ids,
    transform_weight,
    transform_bias,
    norm_gain,
    norm_bias,
    decoder_weight,
    decoder_bias,
    candidates,
    occupancy,
    doc_blocks,
):
    query_count, query_length, model_width = query_states.shape
    vocab_local = decoder_weight.shape[1]
    tile_local, blocks_local, tile_docs, block_terms = doc_blocks.shape
    cand_count = candidates.shape[1]
    term_index = lax.axis_index("term")
    doc_index = lax.axis_index("doc")
    doc_count = lax.axis_size("doc")
    term_count = lax.axis_size("term")
    tile_total = doc_count * tile_local
    hidden = (
        jnp.dot(
            query_states.reshape(query_count * query_length, model_width),
            transform_weight,
            preferred_element_type=jnp.float32,
        )
        + transform_bias
    )
    hidden = jax.nn.gelu(hidden, approximate=False)
    centred = hidden - jnp.mean(hidden, axis=-1, keepdims=True)
    spread = jnp.mean(centred * centred, axis=-1, keepdims=True)
    normed = (centred * lax.rsqrt(spread + 1e-06) * norm_gain + norm_bias).astype(jnp.bfloat16)
    logits = jnp.dot(normed, decoder_weight, preferred_element_type=jnp.float32) + decoder_bias
    activated = jnp.log1p(jnp.maximum(logits, 0.0)).reshape(query_count, query_length, vocab_local)
    live_mask = (token_ids != 0).astype(jnp.float32)[:, :, None]
    columns = term_index * vocab_local + lax.iota(jnp.int32, vocab_local)
    vocab_keep = (columns < VOCAB).astype(jnp.float32)
    weights = (jnp.max(activated * live_mask, axis=1) * vocab_keep).astype(jnp.bfloat16)
    own_hits, own_before = tile_ranks(candidates, tile_total)
    all_weights, all_cand = (
        lax.all_gather(weights, "doc", axis=0, tiled=True),
        lax.all_gather(candidates, "doc", axis=0, tiled=True),
    )
    local_cand = (all_cand - doc_index * tile_local).reshape(doc_count, query_count, cand_count)
    tile_hits, tile_before = tile_ranks(local_cand, tile_local)
    source_row, slot_valid = slot_sources(
        jnp.swapaxes(tile_hits, 1, 2), jnp.swapaxes(tile_before, 1, 2), MOST
    )
    flat_index = lax.iota(jnp.int32, doc_count)[:, None, None] * query_count + source_row
    buffer = jnp.take(all_weights, flat_index.reshape(-1), axis=0).reshape(
        doc_count, tile_local, MOST, vocab_local
    )
    buffer = buffer * slot_valid.astype(jnp.bfloat16)[..., None]
    occupied = occupancy.astype(jnp.bfloat16)
    masked = (
        buffer.reshape(doc_count, tile_local, MOST, blocks_local, block_terms)
        * occupied[None, :, None, :, None]
    )
    partial_value = jnp.einsum(
        "jtrbc,tbdc->jtrd", masked, doc_blocks, preferred_element_type=jnp.float32
    )
    slice_width = tile_docs // term_count
    score_total = lax.psum(partial_value, "term")
    score_share = lax.dynamic_slice_in_dim(score_total, term_index * slice_width, slice_width, 3)
    returned = lax.all_to_all(score_share, "doc", split_axis=0, concat_axis=1, tiled=True)
    slot_rank = jnp.take_along_axis(own_before, candidates, axis=1)
    flat_index = candidates * MOST + slot_rank
    scores = jnp.take(returned.reshape(-1, slice_width), flat_index.reshape(-1), axis=0)
    scores = scores.reshape(query_count, cand_count, slice_width)
    return (weights, scores)


def solution(mesh):
    placed = (
        P("doc", None, None),
        P("doc", None),
        P(),
        P(),
        P(),
        P(),
        P(None, "term"),
        P("term"),
        P("doc", None),
        P("doc", "term"),
        P("doc", "term", None, None),
    )
    return jax.shard_map(
        body,
        mesh=mesh,
        in_specs=placed,
        out_specs=(P("doc", "term"), P("doc", None, "term")),
        check_vma=False,
    )
```

profile of v0, /device:TPU:0, one launch (start us, length us, event | category | flops | bytes accessed | tf_op | source)
XLA Modules:
  0.0 277.1 jit_solution(14397636841789176881)
XLA Ops:
  7.2 0.9 copy.49
  8.2 0.9 copy-done
  9.1 17.7 %fusion.24 = (f32[2048]{0:T(1024)S(1)}, f32[2048,768]{0,1:T(8,128)S(1)}) fusion(f32[768]{0:T(1024)} %param.14, bf16[2048,768]{1,0:T(8,128)(2,1)S(1)} %bitcast.33, bf16[768,768]{1,0:T(8,128)(2,1)} %param.13), kind=kOutput, calls=%fused_computation.66 | convolution fusion | flops 2519726080 | bytes 10628096 | tf_op jit(solution)/shard_map/dot_general | solution.py:50
  26.8 0.7 multiply_reduce_fusion.1
  27.6 26.4 %multiply_reduce_fusion = f32[64,3840]{1,0:T(8,128)S(1)} fusion(f32[64,32]{1,0:T(8,128)S(1)} %compare_convert_fusion, f32[3840]{0:T(1024)S(1)} %copy-done.4, bf16[768,3840]{1,0:T(8,128)(2,1)S(1)} %bitcast.42, f32[2048,768]{0,1:T(8,128)S(1)} %get-tuple-element.7, f32[768]{0:T(1024)S(1)} %copy-done.5, f32[768]{0:T(1024)S(1)} %copy-done.6, ...), kind=kOutput, calls=%fused_computation.3 | convolution fusion | flops 12118671360 | bytes 13218816 | tf_op jit(solution)/shard_map/dot_general | solution.py:61
  54.0 0.8 multiply_convert_fusion
  55.0 6.2 %all-gather = s32[4,64,32]{1,2,0:T(8,128)S(1)} all-gather(s32[1,64,32]{1,2,0:T(8,128)S(1)} %bitcast.38), channel_id=1, replica_groups=mesh['doc'=4,'term'=8] {'doc'}, dimensions={0}, use_global_device_ids=true | all-gather | bytes 40960 | tf_op jit(solution)/shard_map/all_gather | solution.py:70
  61.1 0.1 convert_reduce_fusion
  61.4 0.1 reduce_window_sum.23
  61.6 1.2 select_reduce_fusion
  63.0 1.2 fusion.22
  64.2 15.4 %all-gather.3.cloned.1.call-done = bf16[256,3840]{1,0:T(8,128)(2,1)} async-done(((bf16[64,3840]{1,0:T(8,128)(2,1)}), bf16[256,3840]{1,0:T(8,128)(2,1)}) %all-gather.3.cloned.1.call-update) | async-done | bytes 1966096 | tf_op jit(solution)/shard_map/all_gather | solution.py:69
  79.6 29.7 %gather_fusion = bf16[2048,3840]{1,0:T(8,128)(2,1)} fusion(bf16[256,3840]{1,0:T(8,128)(2,1)} %all-gather.3.cloned.1.call-done, s32[2048]{0:T(1024)S(1)} %broadcast_clamp_fusion.1), kind=kCustom, calls=%fused_computation | custom fusion | bytes 31465472 | tf_op jit(solution)/shard_map/jit(_take)/gather | solution.py:78
  109.3 25.1 %gather.18 = bf16[4,16,32,30,128]{4,3,2,1,0:T(8,128)(2,1)} reshape(bf16[2048,3840]{1,0:T(8,128)(2,1)} %gather_fusion) | data formatting | bytes 31457280 | tf_op jit(solution)/shard_map/jit(_take)/gather | solution.py:78
  134.4 15.3 %multiply_multiply_fusion = bf16[4,16,32,30,128]{4,3,2,1,0:T(8,128)(2,1)} fusion(bf16[4,16,32,30,128]{4,3,2,1,0:T(8,128)(2,1)} %gather.18, pred[4,16,32]{2,1,0:T(8,128)(4,1)S(1)} %get-tuple-element.4, bf16[16,30]{1,0:T(8,128)(2,1)S(1)} %convert_element_type.39, bf16[4,16,32]{2,1,0:T(8,128)(2,1)S(1)} %convert_element_type.38), kind=kLoop, calls=%fused_computation.5 | loop fusion | flops 23592960 | bytes 31464384 | tf_op jit(solution)/shard_map/mul | solution.py:84
  149.8 15.2 %fusion.16 = f32[4,16,32,128]{3,2,0,1:T(8,128)} fusion(bf16[16,30,128,128]{3,2,1,0:T(8,128)(2,1)} %param.21, bf16[4,16,32,30,128]{4,3,2,1,0:T(8,128)(2,1)} %multiply_multiply_fusion), kind=kOutput, calls=%fused_computation.33 | convolution fusion | flops 2013265920 | bytes 32505856 | tf_op jit(solution)/shard_map/jtrbc,tbdc->jtrd/dot_general | solution.py:87
  165.1 0.4 convert_reduce_fusion.1
  165.5 0.1 reduce_window_sum.22
  165.7 13.6 %gather_fusion.2 = s32[2048]{0:T(1024)S(1)} fusion(s32[64,64]{1,0:T(8,128)S(1)} %sub.26, s32[2048]{0:T(1024)S(1)} %reshape.174), kind=kCustom, calls=%fused_computation.2 | custom fusion | bytes 32768 | tf_op jit(solution)/shard_map/jit(take_along_axis)/gather | solution.py:94
  179.5 63.6 %all-reduce.2.cloned.1.call-done = f32[4,16,32,128]{3,2,0,1:T(8,128)} async-done(((f32[4,16,32,128]{3,2,0,1:T(8,128)}), f32[4,16,32,128]{3,2,0,1:T(8,128)}) %all-reduce.2.cloned.1.call-update) | async-done | bytes 1048592 | tf_op jit(solution)/shard_map/psum | solution.py:91
  243.2 1.6 constant_dynamic-slice_fusion
  244.7 0.3 copy.60
  245.1 0.9 reshape.192
  246.0 3.3 %all-to-all-start = ((f32[4,1,8192]{2,1,0:T(1,128)}), f32[4,1,8192]{2,1,0:T(1,128)S(1)}, u32[]{:S(2)}, u32[]{:S(2)}) async-start(f32[4,1,8192]{2,1,0:T(1,128)} %reshape.192), calls=%async_computation | async-start | bytes 262144 | tf_op jit(solution)/shard_map/all_to_all | solution.py:93
  249.4 4.5 %all-to-all-done = f32[4,1,8192]{2,1,0:T(1,128)S(1)} async-done(((f32[4,1,8192]{2,1,0:T(1,128)}), f32[4,1,8192]{2,1,0:T(1,128)S(1)}, u32[]{:S(2)}, u32[]{:S(2)}) %all-to-all-start) | async-done | bytes 131104 | tf_op jit(solution)/shard_map/all_to_all | solution.py:93
  253.9 0.5 broadcast.159
  254.4 1.0 reduce
  255.4 1.0 reshape.193
  256.4 2.5 copy.66
  259.0 8.8 %gather_fusion.1 = f32[2048,16]{1,0:T(8,128)} fusion(f32[2048,16]{1,0:T(8,128)} %bitcast.34, s32[2048]{0:T(1024)S(1)} %broadcast_clamp_fusion), kind=kCustom, calls=%fused_computation.1 | custom fusion | bytes 270336 | tf_op jit(solution)/shard_map/jit(_take)/gather | solution.py:96
  267.7 1.8 copy.63
  269.5 0.7 broadcast_select_fusion
  (48 shorter events, 1.1 us)
Async XLA Ops:
  7.2 1.9 copy-start
  7.2 72.4 %all-gather.3.cloned.1.call-start = ((), (), s32[]{:S(2)}) async-start(), calls=%async_computation.1 | async-start | bytes 2457600 | tf_op jit(solution)/shard_map/all_gather | solution.py:69
  9.1 18.4 %slice-start = ((s8[5898240]{0:T(1024)(128)(4,1)}), s8[4194304]{0:T(1024)(128)(4,1)S(1)}, s32[]{:S(2)}) async-start(s8[5898240]{0:T(1024)(128)(4,1)} %bitcast.41), calls=%async_computation.3 | async-start | bytes 8388608
  9.1 18.4 %slice-start.1 = ((s8[5898240]{0:T(1024)(128)(4,1)}), s8[1703936]{0:T(1024)(128)(4,1)S(1)}, s32[]{:S(2)}) async-start(s8[5898240]{0:T(1024)(128)(4,1)} %bitcast.41), calls=%async_computation.4 | async-start | bytes 3407872
  26.7 0.8 copy-start.4
  26.8 0.8 copy-start.5
  26.8 0.8 copy-start.6
  27.6 27.4 %copy-start.3 = (s32[16,30]{1,0:T(8,128)S(1)}, s32[16,30]{1,0:T(8,128)}, u32[]{:S(2)}) copy-start(s32[16,30]{1,0:T(8,128)} %param.20) | copy-start | bytes 5764
  27.6 27.4 %copy-start.2 = (s32[64,32]{0,1:T(8,128)S(1)}, s32[64,32]{0,1:T(8,128)}, u32[]{:S(2)}) copy-start(s32[64,32]{0,1:T(8,128)} %param.19) | copy-start | bytes 24580
  54.9 188.3 %all-reduce.2.cloned.1.call-start = ((), (), s32[]{:S(2)}) async-start(), calls=%async_computation.2 | async-start | bytes 2097152 | tf_op jit(solution)/shard_map/psum | solution.py:91
  246.0 7.9 %all-to-all-start = ((f32[4,1,8192]{2,1,0:T(1,128)}), f32[4,1,8192]{2,1,0:T(1,128)S(1)}, u32[]{:S(2)}, u32[]{:S(2)}) async-start(f32[4,1,8192]{2,1,0:T(1,128)} %reshape.192), calls=%async_computation | async-start | bytes 262144 | tf_op jit(solution)/shard_map/all_to_all | solution.py:93
  256.4 13.8 %copy-start.1 = (bf16[64,32,768]{2,1,0:T(8,128)(2,1)S(1)}, bf16[64,32,768]{2,1,0:T(8,128)(2,1)}, u32[]{:S(2)}) copy-start(bf16[64,32,768]{2,1,0:T(8,128)(2,1)} %param.11) | copy-start | bytes 9437188
Sparse Core Ops, SparseCore 0:
  55.0 24.5 all-gather.2
  165.2 77.9 all-reduce.1
where the time goes:
time: 278 us; the launch traced here: 277 us
  local copies, waits for them, and re-layouts  88.4 us (32%)
  waiting for transfers between devices  83.5 us (30%)
  matrix products  59.3 us (21%)
  other arithmetic  21.9 us (8%)
  between operations  14.3 us (5%)
  blocking collectives  6.16 us (2%)
  starting transfers between devices  3.41 us (1%)
    psum x1, waiting for transfers between devices, body(): score_total = lax.psum(partial_value, 'term')  63.6 us
    gather x2, local copies, waits for them, and re-layouts, body(): jnp.take(all_weights, flat_index.reshape(-1), axis=0)  54.8 us
    dot_general x1, matrix products, body(): jnp.dot(normed, decoder_weight, preferred_element_type=jnp.float32)  26.4 us
    dot_general x1, matrix products, body(): jnp.dot(query_states.reshape(query_count * query_length, model_width), tr...  17.7 us
    all_gather x1, waiting for transfers between devices, body(): lax.all_gather(weights, 'doc', axis=0, tiled=True)  15.4 us
    mul x1, other arithmetic, body(): buffer.reshape(doc_count, tile_local, MOST, blocks_local, block_terms)  15.3 us
    dot_general x1, matrix products, body(): jnp.einsum('jtrbc,tbdc->jtrd', masked, doc_blocks, preferred_element_type...  15.2 us
    gather x3, local copies, waits for them, and re-layouts, body(): slot_rank = jnp.take_along_axis(own_before, candidates, axis=1)  13.8 us
  transfers between devices with their start and end apart: 3, of which 3 were waited for; matrix products, arithmetic and copies ran while one was open for 6% of the time, Pallas kernels for 0%

commit v1 on v0

v1 whole, which is shorter than its diff:
```python
import functools
import math

import jax
import jax.numpy as jnp
from jax import lax
from jax.experimental import pallas as pl
from jax.experimental.pallas import tpu as pltpu
from jax.sharding import PartitionSpec as P

VOCAB = 30522
MOST = 32
LANES = 128
GROUP = 8
F32 = jnp.float32
BF16 = jnp.bfloat16
WHOLE = pl.BlockSpec(memory_space=pltpu.VMEM)
SCALARS = pl.BlockSpec(memory_space=pltpu.SMEM)


def gelu(value):
    return 0.5 * value * (1.0 + lax.erf(value * math.sqrt(0.5)))


def normed_rows(states, live_at, first, transform, bias, gain, shift):
    queries, length, width = states.shape
    rows = queries * length
    row = lax.broadcasted_iota(jnp.int32, live_at.shape, 0)
    lane = lax.broadcasted_iota(jnp.int32, live_at.shape, 1)
    own = jnp.where(lane == first + row % queries, live_at, 0.0)
    live = jnp.sum(own, axis=1, keepdims=True) > 0.0
    row = lax.broadcasted_iota(jnp.int32, (rows, 1), 0)
    source = row % queries * length + jnp.where(live, row // queries, 0)
    column = lax.broadcasted_iota(jnp.int32, (rows, rows), 1)
    order = jnp.where(column == source, 1.0, 0.0).astype(BF16)
    moved = jnp.dot(order, states.reshape(rows, width), preferred_element_type=F32)
    hidden = jnp.dot(moved.astype(BF16), transform, preferred_element_type=F32)
    hidden = gelu(hidden + bias)
    centred = hidden - jnp.mean(hidden, axis=1, keepdims=True)
    spread = jnp.mean(centred * centred, axis=1, keepdims=True)
    return (centred * lax.rsqrt(spread + 1e-06) * gain + shift).astype(BF16)


def expand_kernel(
    piece,
    start_ref,
    states_ref,
    tokens_ref,
    transform_ref,
    bias_ref,
    gain_ref,
    shift_ref,
    decoder_ref,
    decoder_bias_ref,
    cand_ref,
    out_ref,
    pooled,
):
    length, query_total = tokens_ref.shape
    vocab = decoder_ref.shape[1]
    rows = GROUP * length
    at = lax.broadcasted_iota(jnp.int32, (rows, length), 0) // GROUP
    spot = lax.broadcasted_iota(jnp.int32, (rows, length), 1)
    pick = jnp.where(at == spot, 1.0, 0.0).astype(BF16)
    alive = jnp.where(tokens_ref[...] != 0, 1.0, 0.0).astype(BF16)
    live_at = jnp.dot(pick, alive, preferred_element_type=F32)
    count = out_ref.shape[0]
    step = 768 if vocab % 768 == 0 else 640
    for group in range(count // GROUP):
        first = piece * count + group * GROUP
        normed = normed_rows(
            states_ref[first : first + GROUP],
            live_at,
            first,
            transform_ref[...],
            bias_ref[...],
            gain_ref[...],
            shift_ref[...],
        )
        for begin in range(0, vocab, step):
            part = slice(begin, begin + step)
            logits = jnp.dot(normed, decoder_ref[:, part], preferred_element_type=F32)
            top = jnp.max(logits.reshape(length, GROUP, step), axis=0)
            top = jnp.log1p(jnp.maximum(top + decoder_bias_ref[:, part], 0.0))
            pooled[group * GROUP : (group + 1) * GROUP, part] = top
    column = start_ref[0] + lax.broadcasted_iota(jnp.int32, (count, vocab), 1)
    out_ref[:, :vocab] = jnp.where(column < VOCAB, pooled[...], 0.0).astype(BF16)
    if out_ref.shape[1] > vocab:
        wide = jnp.zeros((count, LANES), F32)
        wide = jnp.concatenate(
            [cand_ref[...].astype(F32), jnp.zeros((count, LANES - query_total), F32)], axis=1
        )
        out_ref[:, vocab:] = wide.astype(BF16)


def ranks(cand, tiles, base):
    depth, total = cand.shape
    row = lax.broadcasted_iota(jnp.int32, (tiles, total), 0) + base
    hits = jnp.zeros((tiles, total), F32)
    for place in range(depth):
        hits = jnp.where(cand[place : place + 1, :] == row, 1.0, hits)
    earlier = lax.broadcasted_iota(jnp.int32, (total, total), 0)
    later = lax.broadcasted_iota(jnp.int32, (total, total), 1)
    block = 64
    ahead = (earlier < later) & (earlier // block == later // block)
    before = jnp.dot(
        hits.astype(BF16), jnp.where(ahead, 1.0, 0.0).astype(BF16), preferred_element_type=F32
    )
    return jnp.where(hits > 0.0, before, -1.0)


def score_kernel(parties, pieces, place_ref, occupancy_ref, docs_ref, *refs):
    piece_refs = refs[: parties * pieces]
    out_ref, turned, rank, total = refs[parties * pieces :]
    step = pl.program_id(0)
    tiles, blocks, docs, terms = docs_ref.shape
    vocab = blocks * terms
    term_count = out_ref.shape[1]
    share = docs // term_count
    each = piece_refs[0].shape[0]
    queries = each * pieces

    @pl.when(step == 0)
    def _():
        cands = []
        for party in range(parties):
            weights = jnp.concatenate(
                [piece_refs[party * pieces + k][:, :vocab] for k in range(pieces)], axis=0
            )
            cands.append(piece_refs[party * pieces][:, vocab : vocab + queries].astype(F32))
            turned[party * queries : (party + 1) * queries, :] = weights
        cand = jnp.concatenate(cands, axis=1).astype(jnp.int32)
        rank[...] = ranks(cand, rank.shape[0], place_ref[0] * rank.shape[0])

    rows = []
    for tile in range(tiles):
        row = [
            jnp.where(occupancy_ref[step * tiles + tile, block] != 0, docs_ref[tile, block], 0.0).astype(BF16)
            for block in range(blocks)
        ]
        rows.append(jnp.concatenate(row, axis=1))
    left = jnp.concatenate(rows, axis=0)
    value = lax.dot_general(
        left, turned[...], (((1,), (1,)), ((), ())), preferred_element_type=F32
    ).astype(BF16)
    all_queries = parties * queries
    slot = lax.broadcasted_iota(jnp.int32, (parties * LANES, all_queries), 0)
    owner = lax.broadcasted_iota(jnp.int32, (parties * LANES, all_queries), 1) // queries
    chosen = jnp.zeros((docs, parties * LANES), F32)
    for tile in range(tiles):
        want = rank[pl.ds(step * tiles + tile, 1), :].astype(jnp.int32)
        want = jnp.where(want >= 0, want + tile * MOST, -1)
        goal = jnp.where(want >= 0, want + owner * LANES, -1)
        hot = jnp.where(slot == goal, 1.0, 0.0).astype(BF16)
        chosen = chosen + lax.dot_general(
            value[tile * docs : (tile + 1) * docs],
            hot,
            (((1,), (1,)), ((), ())),
            preferred_element_type=F32,
        )
    for party in range(parties):
        part = chosen[:, party * LANES : (party + 1) * LANES]
        for term in range(term_count):
            total[party, term, pl.ds(step * share, share), :] = part[term * share : (term + 1) * share]

    @pl.when(step == pl.num_programs(0) - 1)
    def _():
        for party in range(parties):
            out_ref[place_ref[0] ^ party] = total[party].astype(BF16)


def final_kernel(cand_ref, got_ref, out_ref):
    docs_n, term_count, rows, _ = got_ref.shape
    depth, share, queries = out_ref.shape
    groups = rows // share
    tiles = LANES // MOST
    all_tiles = docs_n * groups * tiles
    cand = cand_ref[...]
    rank = ranks(cand, all_tiles, 0)
    slot = lax.broadcasted_iota(jnp.int32, (LANES, tiles * queries), 0)
    twice = jnp.concatenate([cand, cand], axis=1)
    lane = lax.broadcasted_iota(jnp.int32, (1, 2 * queries), 1) // queries
    result = [jnp.zeros((share, 2 * queries), F32) for _ in range(depth)]
    for doc in range(docs_n):
        summed = got_ref[doc, 0].astype(F32)
        for term in range(1, term_count):
            summed = summed + got_ref[doc, term].astype(F32)
        for group in range(groups):
            first = (doc * groups + group) * tiles
            want = jnp.concatenate(
                [
                    jnp.where(rank[first + k : first + k + 1] >= 0.0, rank[first + k : first + k + 1] + k * MOST, -1.0)
                    for k in range(tiles)
                ],
                axis=1,
            ).astype(jnp.int32)
            hot = jnp.where(slot == want, 1.0, 0.0).astype(BF16)
            value = summed[group * share : (group + 1) * share]
            high = value.astype(BF16)
            low = (value - high.astype(F32)).astype(BF16)
            moved = jnp.dot(high, hot, preferred_element_type=F32) + jnp.dot(
                low, hot, preferred_element_type=F32
            )
            for pair in range(tiles // 2):
                held = moved[:, pair * 2 * queries : (pair + 1) * 2 * queries]
                name = first + pair * 2 + lane
                for place in range(depth):
                    result[place] = jnp.where(twice[place : place + 1] == name, held, result[place])
    for place in range(depth):
        out_ref[place] = result[place][:, :queries] + result[place][:, queries:]


def body(
    query_states,
    token_ids,
    transform_weight,
    transform_bias,
    norm_gain,
    norm_bias,
    decoder_weight,
    decoder_bias,
    candidates,
    occupancy,
    doc_blocks,
):
    query_count, length, width = query_states.shape
    vocab = decoder_weight.shape[1]
    tile_local, blocks, docs, terms = doc_blocks.shape
    depth = candidates.shape[1]
    term_index, doc_index = lax.axis_index("term"), lax.axis_index("doc")
    doc_count, term_count = lax.axis_size("doc"), lax.axis_size("term")
    pieces = 2
    each = query_count // pieces
    share = docs // term_count
    cand = candidates.T
    start = (term_index * vocab).reshape(1)
    place = doc_index.reshape(1)

    own = []
    for piece in range(pieces):
        wide = vocab + (LANES if piece == 0 else 0)
        own.append(
            pl.pallas_call(
                functools.partial(expand_kernel, piece),
                in_specs=[SCALARS] + [WHOLE] * 9,
                out_specs=WHOLE,
                out_shape=jax.ShapeDtypeStruct((each, wide), BF16),
                scratch_shapes=[pltpu.VMEM((each, vocab), F32)],
                cost_estimate=pl.CostEstimate(
                    flops=2 * each * length * width * (vocab + width), bytes_accessed=10**7, transcendentals=0
                ),
                compiler_params=pltpu.CompilerParams(vmem_limit_bytes=24 << 20),
                name="expand",
            )(
                start,
                query_states,
                token_ids.T,
                transform_weight,
                transform_bias.reshape(1, -1),
                norm_gain.reshape(1, -1),
                norm_bias.reshape(1, -1),
                decoder_weight,
                decoder_bias.reshape(1, -1),
                cand,
            )
        )

    held = [[None] * pieces for _ in range(doc_count)]
    for piece in range(pieces):
        held[0][piece] = own[piece]
        bit = doc_count // 2
        known = [0]
        while bit:
            swap = [(i, i ^ bit) for i in range(doc_count)]
            for k in list(known):
                held[k | bit][piece] = lax.ppermute(held[k][piece], "doc", swap)
                known.append(k | bit)
            bit //= 2
    weights = jnp.concatenate([own[0][:, :vocab], own[1]], axis=0)

    tiles = LANES // MOST
    steps = tile_local // tiles
    all_queries = doc_count * query_count
    sent = pl.pallas_call(
        functools.partial(score_kernel, doc_count, pieces),
        grid=(steps,),
        in_specs=[SCALARS, SCALARS, pl.BlockSpec((tiles, blocks, docs, terms), lambda i: (i, 0, 0, 0))]
        + [WHOLE] * (doc_count * pieces),
        out_specs=pl.BlockSpec((doc_count, term_count, steps * share, LANES), lambda i: (0, 0, 0, 0)),
        out_shape=jax.ShapeDtypeStruct((doc_count, term_count, steps * share, LANES), BF16),
        scratch_shapes=[
            pltpu.VMEM((all_queries, vocab), BF16),
            pltpu.VMEM((tile_local, all_queries), F32),
            pltpu.VMEM((doc_count, term_count, steps * share, LANES), F32),
        ],
        cost_estimate=pl.CostEstimate(
            flops=2 * tile_local * docs * vocab * all_queries, bytes_accessed=2 * 10**7, transcendentals=0
        ),
        compiler_params=pltpu.CompilerParams(vmem_limit_bytes=36 << 20),
        name="score",
    )(place, occupancy, doc_blocks, *[held[k][piece] for k in range(doc_count) for piece in range(pieces)])

    everyone = doc_count * term_count
    got = lax.all_to_all(
        sent.reshape(everyone, steps * share, LANES), ("doc", "term"), split_axis=0, concat_axis=0, tiled=True
    ).reshape(doc_count, term_count, steps * share, LANES)

    scores = pl.pallas_call(
        final_kernel,
        in_specs=[WHOLE, WHOLE],
        out_specs=WHOLE,
        out_shape=jax.ShapeDtypeStruct((depth, share, query_count), F32),
        compiler_params=pltpu.CompilerParams(vmem_limit_bytes=24 << 20),
        name="place",
    )(cand, got)
    return weights, scores.transpose(2, 0, 1)


def solution(mesh):
    placed = (
        P("doc", None, None),
        P("doc", None),
        P(),
        P(),
        P(),
        P(),
        P(None, "term"),
        P("term"),
        P("doc", None),
        P("doc", "term"),
        P("doc", "term", None, None),
    )
    return jax.shard_map(
        body,
        mesh=mesh,
        in_specs=placed,
        out_specs=(P("doc", "term"), P("doc", None, "term")),
        check_vma=False,
    )
```

time: 278 us -> 83.7 us (0.30)
  local copies, waits for them, and re-layouts: 88.4 us -> 15.6 us
  waiting for transfers between devices: 83.5 us -> 23.8 us
  matrix products: 59.3 us -> 0 us
  Pallas kernels: 0 us -> 33.5 us
  other arithmetic: 21.9 us -> 0.81 us
  between operations: 14.3 us -> 0.72 us
  blocking collectives: 6.16 us -> 0 us
  starting transfers between devices: 3.41 us -> 8.65 us
    gather x7 -> x0, local copies, waits for them, and re-layouts: 79.2 us -> none  [the longest x2 54.8 us: body(): jnp.take(all_weights, flat_index.reshape(-1), axis=0)]
    psum x1 -> x0, waiting for transfers between devices: 63.6 us -> none  [body(): score_total = lax.psum(partial_value, 'term')]
    dot_general x3 -> x0, matrix products: 59.3 us -> none  [the longest x1 26.4 us: body(): jnp.dot(normed, decoder_weight, preferred_element_type=jnp.float32)]
    pallas_call x0 -> x4, Pallas kernels: none -> 33.5 us  [the longest x2 21 us: body(): pl.pallas_call(functools.partial(expand_kernel, piece), in_specs=[SCALARS...]
    all_gather x1 -> x0, waiting for transfers between devices: 15.4 us -> none  [body(): lax.all_gather(weights, 'doc', axis=0, tiled=True)]
    mul x2 -> x0, other arithmetic: 15.3 us -> none  [the longest x1 15.3 us: body(): buffer.reshape(doc_count, tile_local, MOST, blocks_local, block_terms)]
    all_to_all x1, waiting for transfers between devices: 4.5 us -> 15.5 us  [body(): lax.all_to_all(sent.reshape(everyone, steps * share, LANES), ('doc', 'ter...]
    unnamed x22 -> x16, local copies, waits for them, and re-layouts: 3.88 us -> 12.7 us
  transfers between devices with their start and end apart: 3 -> 7, of which waited for: 3 -> 3; matrix products, arithmetic and copies ran while one was open for 6% -> 1% of each run, Pallas kernels for 0% -> 13%
where the time goes in v1:
time: 83.7 us; the launch traced here: 83 us
  Pallas kernels  33.5 us (40%)
  waiting for transfers between devices  23.8 us (28%)
  local copies, waits for them, and re-layouts  15.6 us (19%)
  starting transfers between devices  8.65 us (10%)
    pallas_call x2, Pallas kernels, body(): pl.pallas_call(functools.partial(expand_kernel, piece), in_specs=[SCALARS...  21 us
    all_to_all x1, waiting for transfers between devices, body(): lax.all_to_all(sent.reshape(everyone, steps * share, LANES), ('doc', 'ter...  15.5 us
    unnamed x16, local copies, waits for them, and re-layouts  12.7 us
    pallas_call x1, Pallas kernels, body(): pl.pallas_call(functools.partial(score_kernel, doc_count, pieces), grid=(...  10.3 us
    ppermute x6, waiting for transfers between devices, body(): held[k | bit][piece] = lax.ppermute(held[k][piece], 'doc', swap)  8.27 us
    all_to_all x1, starting transfers between devices, body(): lax.all_to_all(sent.reshape(everyone, steps * share, LANES), ('doc', 'ter...  4.92 us
    ppermute x6, starting transfers between devices, body(): held[k | bit][piece] = lax.ppermute(held[k][piece], 'doc', swap)  3.72 us
    pallas_call x1, Pallas kernels, body(): pl.pallas_call(final_kernel, in_specs=[WHOLE, WHOLE], out_specs=WHOLE, ou...  2.19 us
  transfers between devices with their start and end apart: 7, of which 3 were waited for; matrix products, arithmetic and copies ran while one was open for 1% of the time, Pallas kernels for 13%

profile of v1, /device:TPU:0, one launch (start us, length us, event | category | flops | bytes accessed | tf_op | source)
XLA Modules:
  0.0 83.0 jit_solution(834826533031197641)
XLA Ops:
  0.6 0.7 reshape.36.decoder_bias_ref
  1.4 0.7 reshape.33.bias_ref
  2.1 0.7 reshape.34.gain_ref
  2.7 0.7 reshape.35.shift_ref
  3.4 0.7 copy-done.1
  4.2 2.7 %copy-done.4 = bf16[768,3840]{1,0:T(8,128)(2,1)S(1)} copy-done((bf16[768,3840]{1,0:T(8,128)(2,1)S(1)}, bf16[768,3840]{1,0:T(8,128)(2,1)}, u32[]{:S(2)}) %copy-start.4) | copy-done | bytes 5898264
  6.8 1.9 %copy-done.5 = bf16[64,32,768]{2,1,0:T(8,128)(2,1)S(1)} copy-done((bf16[64,32,768]{2,1,0:T(8,128)(2,1)S(1)}, bf16[64,32,768]{2,1,0:T(8,128)(2,1)}, u32[]{:S(2)}) %copy-start.5) | copy-done | bytes 3145752
  8.7 1.3 %copy-done.6 = bf16[768,768]{1,0:T(8,128)(2,1)S(1)} copy-done((bf16[768,768]{1,0:T(8,128)(2,1)S(1)}, bf16[768,768]{1,0:T(8,128)(2,1)}, u32[]{:S(2)}) %copy-start.6) | copy-done | bytes 1179672
  10.0 0.7 copy-done.7
  10.7 10.4 %expand.2.refs_0_ = bf16[32,3968]{1,0:T(8,128)(2,1)S(1)} custom-call(s32[1]{0:T(128)} %bitcast.start_ref, bf16[64,32,768]{2,1,0:T(8,128)(2,1)S(1)} %copy-done.5, s32[32,64]{1,0:T(8,128)S(1)} %bitcast.11, bf16[768,768]{1,0:T(8,128)(2,1)S(1)} %copy-done.6, f32[1,768]{1,0:T(1,128)S(1)} %reshape.33.bias_ref, f32[1,768]{1,0:T(1,128)S(1)} %reshape.34.gain_ref, ...), custom_call_target="tpu_custom_call" | custom-call | flops 7247757312 | bytes 10000000 | tf_op jit(solution)/shard_map/expand/pallas_call | solution.py:243
  21.1 0.0 copy-start.3
  21.1 3.0 %collective-permute-start.2 = (bf16[32,3968]{1,0:T(8,128)(2,1)S(1)}, bf16[32,3968]{1,0:T(8,128)(2,1)S(1)}, u32[]{:S(2)}, u32[]{:S(2)}) collective-permute-start(bf16[32,3968]{1,0:T(8,128)(2,1)S(1)} %expand.2.refs_0_), channel_id=1, source_target_pairs={{0,16},{8,24},{16,0},{24,8},{1,17},{9,25},{17,1},{25,9},{2,18},{10... | collective-permute-start | bytes 761864 | tf_op jit(solution)/shard_map/ppermute | solution.py:276
  24.1 10.6 %expand.3.refs_1_ = bf16[32,3840]{1,0:T(8,128)(2,1)S(1)} custom-call(s32[1]{0:T(128)} %bitcast.start_ref, bf16[64,32,768]{2,1,0:T(8,128)(2,1)S(1)} %copy-done.5, s32[32,64]{1,0:T(8,128)S(1)} %bitcast.12, bf16[768,768]{1,0:T(8,128)(2,1)S(1)} %copy-done.6, f32[1,768]{1,0:T(1,128)S(1)} %reshape.33.bias_ref, f32[1,768]{1,0:T(1,128)S(1)} %reshape.34.gain_ref, ...), custom_call_target="tpu_custom_call" | custom-call | flops 7247757312 | bytes 10000000 | tf_op jit(solution)/shard_map/expand/pallas_call | solution.py:243
  34.7 0.1 collective-permute-start.3
  34.8 0.1 collective-permute-start
  34.9 0.0 collective-permute-done.2.refs_4_
  34.9 0.5 collective-permute-start.4
  35.4 0.1 collective-permute-start.1
  35.5 6.8 %collective-permute-done.3.refs_5_ = bf16[32,3840]{1,0:T(8,128)(2,1)S(1)} collective-permute-done((bf16[32,3840]{1,0:T(8,128)(2,1)S(1)}, bf16[32,3840]{1,0:T(8,128)(2,1)S(1)}, u32[]{:S(2)}, u32[]{:S(2)}) %collective-permute-start.3) | collective-permute-done | bytes 245792 | tf_op jit(solution)/shard_map/ppermute | solution.py:276
  42.2 0.0 collective-permute-start.5
  42.2 0.0 collective-permute-done.1.refs_3_
  42.2 0.0 collective-permute-done.refs_2_
  42.2 1.5 %collective-permute-done.5.refs_7_ = bf16[32,3840]{1,0:T(8,128)(2,1)S(1)} collective-permute-done((bf16[32,3840]{1,0:T(8,128)(2,1)S(1)}, bf16[32,3840]{1,0:T(8,128)(2,1)S(1)}, u32[]{:S(2)}, u32[]{:S(2)}) %collective-permute-start.5) | collective-permute-done | bytes 245792 | tf_op jit(solution)/shard_map/ppermute | solution.py:276
  43.7 0.0 collective-permute-done.4.refs_6_
  43.7 0.0 copy-done.3
  43.7 5.5 %copy-done = bf16[16,30,128,128]{3,2,1,0:T(8,128)(2,1)S(1)} copy-done((bf16[16,30,128,128]{3,2,1,0:T(8,128)(2,1)S(1)}, bf16[16,30,128,128]{3,2,1,0:T(8,128)(2,1)}, u32[]{:S(2)}) %copy-start) | copy-done | bytes 15728664
  49.2 10.3 %score.1 = bf16[4,8,64,128]{3,2,1,0:T(8,128)(2,1)} custom-call(s32[1]{0:T(128)} %bitcast.3.place_ref, s32[16,30]{1,0:T(8,128)S(1)} %copy-done.3, bf16[16,30,128,128]{3,2,1,0:T(8,128)(2,1)S(1)} %copy-done, bf16[32,3968]{1,0:T(8,128)(2,1)S(1)} %expand.2.refs_0_, bf16[32,3840]{1,0:T(8,128)(2,1)S(1)} %expand.3.refs_1_, ...), custom_call_target="tpu_custom_call" | custom-call | flops 4026531840 | bytes 20000000 | tf_op jit(solution)/shard_map/score/pallas_call | solution.py:284
  59.5 4.9 %all-to-all-start = ((bf16[32,64,128]{2,1,0:T(8,128)(2,1)}), bf16[32,64,128]{2,1,0:T(8,128)(2,1)S(1)}, u32[]{:S(2)}, u32[]{:S(2)}) async-start(bf16[32,64,128]{2,1,0:T(8,128)(2,1)} %bitcast.4), calls=%async_computation | async-start | bytes 1048576 | tf_op jit(solution)/shard_map/all_to_all | solution.py:304
  64.5 0.8 pad_maximum_fusion
  65.3 15.5 %all-to-all-done = bf16[32,64,128]{2,1,0:T(8,128)(2,1)S(1)} async-done(((bf16[32,64,128]{2,1,0:T(8,128)(2,1)}), bf16[32,64,128]{2,1,0:T(8,128)(2,1)S(1)}, u32[]{:S(2)}, u32[]{:S(2)}) %all-to-all-start) | async-done | bytes 524320 | tf_op jit(solution)/shard_map/all_to_all | solution.py:304
  80.8 0.0 copy-done.2
  80.8 2.2 %place.1 = f32[32,16,64]{2,1,0:T(8,128)} custom-call(s32[32,64]{1,0:T(8,128)S(1)} %bitcast.10, bf16[4,8,64,128]{3,2,1,0:T(8,128)(2,1)S(1)} %bitcast.7), custom_call_target="tpu_custom_call" | custom-call | tf_op jit(solution)/shard_map/place/pallas_call | solution.py:308
  (8 shorter events, 0.0 us)
Async XLA Ops:
  3.4 0.7 copy-start.1
  4.2 2.7 %copy-start.4 = (bf16[768,3840]{1,0:T(8,128)(2,1)S(1)}, bf16[768,3840]{1,0:T(8,128)(2,1)}, u32[]{:S(2)}) copy-start(bf16[768,3840]{1,0:T(8,128)(2,1)} %decoder_ref.3) | copy-start | bytes 17694724
  6.8 1.9 %copy-start.5 = (bf16[64,32,768]{2,1,0:T(8,128)(2,1)S(1)}, bf16[64,32,768]{2,1,0:T(8,128)(2,1)}, u32[]{:S(2)}) copy-start(bf16[64,32,768]{2,1,0:T(8,128)(2,1)} %states_ref.3) | copy-start | bytes 9437188
  8.7 1.3 %copy-start.6 = (bf16[768,768]{1,0:T(8,128)(2,1)S(1)}, bf16[768,768]{1,0:T(8,128)(2,1)}, u32[]{:S(2)}) copy-start(bf16[768,768]{1,0:T(8,128)(2,1)} %transform_ref.3) | copy-start | bytes 3538948
  10.0 0.7 copy-start.7
  21.1 22.6 %copy-start.3 = (s32[16,30]{1,0:T(8,128)S(1)}, s32[16,30]{1,0:T(8,128)}, u32[]{:S(2)}) copy-start(s32[16,30]{1,0:T(8,128)} %occupancy_ref.1) | copy-start | bytes 5764
  21.1 13.8 %collective-permute-start.2 = (bf16[32,3968]{1,0:T(8,128)(2,1)S(1)}, bf16[32,3968]{1,0:T(8,128)(2,1)S(1)}, u32[]{:S(2)}, u32[]{:S(2)}) collective-permute-start(bf16[32,3968]{1,0:T(8,128)(2,1)S(1)} %expand.2.refs_0_), channel_id=1, source_target_pairs={{0,16},{8,24},{16,0},{24,8},{1,17},{9,25},{17,1},{25,9},{2,18},{10... | collective-permute-start | bytes 761864 | tf_op jit(solution)/shard_map/ppermute | solution.py:276
  34.7 7.5 %collective-permute-start.3 = (bf16[32,3840]{1,0:T(8,128)(2,1)S(1)}, bf16[32,3840]{1,0:T(8,128)(2,1)S(1)}, u32[]{:S(2)}, u32[]{:S(2)}) collective-permute-start(bf16[32,3840]{1,0:T(8,128)(2,1)S(1)} %expand.3.refs_1_), channel_id=1, source_target_pairs={{0,16},{8,24},{16,0},{24,8},{1,17},{9,25},{17,1},{25,9},{2,18},{10... | collective-permute-start | bytes 737288 | tf_op jit(solution)/shard_map/ppermute | solution.py:276
  34.8 7.4 %collective-permute-start = (bf16[32,3968]{1,0:T(8,128)(2,1)S(1)}, bf16[32,3968]{1,0:T(8,128)(2,1)S(1)}, u32[]{:S(2)}, u32[]{:S(2)}) collective-permute-start(bf16[32,3968]{1,0:T(8,128)(2,1)S(1)} %expand.2.refs_0_), channel_id=1, source_target_pairs={{0,8},{8,0},{16,24},{24,16},{1,9},{9,1},{17,25},{25,17},{2,10},{10... | collective-permute-start | bytes 761864 | tf_op jit(solution)/shard_map/ppermute | solution.py:276
  34.9 8.9 %collective-permute-start.4 = (bf16[32,3968]{1,0:T(8,128)(2,1)S(1)}, bf16[32,3968]{1,0:T(8,128)(2,1)S(1)}, u32[]{:S(2)}, u32[]{:S(2)}) collective-permute-start(bf16[32,3968]{1,0:T(8,128)(2,1)S(1)} %collective-permute-done.2.refs_4_), channel_id=1, source_target_pairs={{0,8},{8,0},{16,24},{24,16},{1,9},{9,1},{17,25},{25,17},{2,10},{10... | collective-permute-start | bytes 761864 | tf_op jit(solution)/shard_map/ppermute | solution.py:276
  35.4 6.9 %collective-permute-start.1 = (bf16[32,3840]{1,0:T(8,128)(2,1)S(1)}, bf16[32,3840]{1,0:T(8,128)(2,1)S(1)}, u32[]{:S(2)}, u32[]{:S(2)}) collective-permute-start(bf16[32,3840]{1,0:T(8,128)(2,1)S(1)} %expand.3.refs_1_), channel_id=1, source_target_pairs={{0,8},{8,0},{16,24},{24,16},{1,9},{9,1},{17,25},{25,17},{2,10},{10... | collective-permute-start | bytes 737288 | tf_op jit(solution)/shard_map/ppermute | solution.py:276
  42.2 1.5 %collective-permute-start.5 = (bf16[32,3840]{1,0:T(8,128)(2,1)S(1)}, bf16[32,3840]{1,0:T(8,128)(2,1)S(1)}, u32[]{:S(2)}, u32[]{:S(2)}) collective-permute-start(bf16[32,3840]{1,0:T(8,128)(2,1)S(1)} %collective-permute-done.3.refs_5_), channel_id=1, source_target_pairs={{0,8},{8,0},{16,24},{24,16},{1,9},{9,1},{17,25},{25,17},{2,10},{10... | collective-permute-start | bytes 737288 | tf_op jit(solution)/shard_map/ppermute | solution.py:276
  43.7 5.5 %copy-start = (bf16[16,30,128,128]{3,2,1,0:T(8,128)(2,1)S(1)}, bf16[16,30,128,128]{3,2,1,0:T(8,128)(2,1)}, u32[]{:S(2)}) copy-start(bf16[16,30,128,128]{3,2,1,0:T(8,128)(2,1)} %docs_ref.1) | copy-start | bytes 47185924
  49.2 31.6 %copy-start.2 = (s32[64,32]{0,1:T(8,128)S(1)}, s32[64,32]{0,1:T(8,128)}, u32[]{:S(2)}) copy-start(s32[64,32]{0,1:T(8,128)} %param.19) | copy-start | bytes 24580
  59.5 21.3 %all-to-all-start = ((bf16[32,64,128]{2,1,0:T(8,128)(2,1)}), bf16[32,64,128]{2,1,0:T(8,128)(2,1)S(1)}, u32[]{:S(2)}, u32[]{:S(2)}) async-start(bf16[32,64,128]{2,1,0:T(8,128)(2,1)} %bitcast.4), calls=%async_computation | async-start | bytes 1048576 | tf_op jit(solution)/shard_map/all_to_all | solution.py:304

commit v2 on v1

v2 whole, which is shorter than its diff:
```python
import functools
import math

import jax
import jax.numpy as jnp
from jax import lax
from jax.experimental import pallas as pl
from jax.experimental.pallas import tpu as pltpu
from jax.sharding import PartitionSpec as P

VOCAB = 30522
MOST = 32
LANES = 128
GROUP = 8
F32 = jnp.float32
BF16 = jnp.bfloat16
WHOLE = pl.BlockSpec(memory_space=pltpu.VMEM)
FAR = pl.BlockSpec(memory_space=pltpu.HBM)
LIMIT = 8 << 20
SCALARS = pl.BlockSpec(memory_space=pltpu.SMEM)


def gelu(value):
    return 0.5 * value * (1.0 + lax.erf(value * math.sqrt(0.5)))


def normed_rows(states, live_at, first, transform, bias, gain, shift):
    queries, length, width = states.shape
    rows = queries * length
    row = lax.broadcasted_iota(jnp.int32, live_at.shape, 0)
    lane = lax.broadcasted_iota(jnp.int32, live_at.shape, 1)
    own = jnp.where(lane == first + row % queries, live_at, 0.0)
    live = jnp.sum(own, axis=1, keepdims=True) > 0.0
    row = lax.broadcasted_iota(jnp.int32, (rows, 1), 0)
    source = row % queries * length + jnp.where(live, row // queries, 0)
    column = lax.broadcasted_iota(jnp.int32, (rows, rows), 1)
    order = jnp.where(column == source, 1.0, 0.0).astype(BF16)
    moved = jnp.dot(order, states.reshape(rows, width), preferred_element_type=F32)
    hidden = jnp.dot(moved.astype(BF16), transform, preferred_element_type=F32)
    hidden = gelu(hidden + bias)
    centred = hidden - jnp.mean(hidden, axis=1, keepdims=True)
    spread = jnp.mean(centred * centred, axis=1, keepdims=True)
    return (centred * lax.rsqrt(spread + 1e-06) * gain + shift).astype(BF16)


def place_of(rows, live_at, tokens_ref):
    length = tokens_ref.shape[0]
    at = lax.broadcasted_iota(jnp.int32, (rows, length), 0) // GROUP
    spot = lax.broadcasted_iota(jnp.int32, (rows, length), 1)
    pick = jnp.where(at == spot, 1.0, 0.0).astype(BF16)
    alive = jnp.where(tokens_ref[...] != 0, 1.0, 0.0).astype(BF16)
    live_at[...] = jnp.dot(pick, alive, preferred_element_type=F32)


def pool(rows, decoder_ref, bias_ref, group, length, out_ref):
    logits = jnp.dot(rows, decoder_ref[...], preferred_element_type=F32)
    top = jnp.max(logits.reshape(length, GROUP, logits.shape[1]), axis=0)
    out_ref[group * GROUP : (group + 1) * GROUP, :] = jnp.log1p(
        jnp.maximum(top + bias_ref[...], 0.0)
    )


def keep_vocab(start, pooled):
    column = start + lax.broadcasted_iota(jnp.int32, pooled.shape, 1)
    return jnp.where(column < VOCAB, pooled[...], 0.0).astype(BF16)


def first_kernel(
    start_ref,
    states_hbm,
    tokens_hbm,
    transform_hbm,
    bias_hbm,
    gain_hbm,
    shift_hbm,
    decoder_hbm,
    decoder_bias_hbm,
    cand_hbm,
    out_ref,
    normed_ref,
    next_ref,
    decoder_bias_ref,
    states_ref,
    transform_ref,
    decoder_ref,
    bias_ref,
    gain_ref,
    shift_ref,
    tokens_ref,
    cand_ref,
    live_at,
    pooled,
    sems,
):
    queries, length, _ = states_ref.shape
    groups = queries // GROUP
    rows = GROUP * length
    chunk = decoder_ref.shape[1]
    always = start_ref[0] >= 0
    copies = []

    def bring(source, target):
        copy = pltpu.make_async_copy(source, target, sems.at[len(copies)])
        copies.append(copy)
        copy.start()

    half = pl.ds(0, 2 * GROUP)
    other = pl.ds(2 * GROUP, queries - 2 * GROUP)
    bring(tokens_hbm, tokens_ref)
    bring(bias_hbm, bias_ref.at[0])
    bring(gain_hbm, gain_ref.at[0])
    bring(shift_hbm, shift_ref.at[0])
    bring(states_hbm.at[half], states_ref.at[half])
    bring(transform_hbm, transform_ref)
    early = len(copies)
    bring(decoder_hbm.at[:, pl.ds(0, chunk)], decoder_ref)
    for at in range(decoder_bias_ref.shape[0]):
        bring(decoder_bias_hbm.at[pl.ds(at * chunk, chunk)], decoder_bias_ref.at[at, 0])
    bring(states_hbm.at[other], states_ref.at[other])
    bring(cand_hbm, cand_ref)
    middle = len(copies)

    def normed(group):
        at = group * GROUP
        normed_ref[group * rows : (group + 1) * rows, :] = normed_rows(
            states_ref[at : at + GROUP],
            live_at[...],
            at,
            transform_ref[...],
            bias_ref[...],
            gain_ref[...],
            shift_ref[...],
        )

    for copy in copies[:early]:
        copy.wait()

    @pl.when(always)
    def _():
        place_of(rows, live_at, tokens_ref)
        normed(0)

    for copy in copies[early:middle]:
        copy.wait()
    bring(decoder_hbm.at[:, pl.ds(chunk, chunk)], next_ref)

    @pl.when(always)
    def _():
        for group in range(groups):
            if group + 1 < groups:
                normed(group + 1)
            part = normed_ref[group * rows : (group + 1) * rows, :]
            pool(part, decoder_ref, decoder_bias_ref[0], group, length, pooled)
        out_ref[:, :chunk] = keep_vocab(start_ref[0], pooled)
        depth = cand_ref.shape[0]
        wide = jnp.concatenate([cand_ref[...].astype(F32), jnp.zeros((depth, LANES - queries), F32)], axis=1)
        if depth < queries:
            wide = jnp.concatenate([wide, jnp.zeros((queries - depth, LANES), F32)], axis=0)
        out_ref[:, chunk:] = wide.astype(BF16)

    copies[-1].wait()


def chunk_kernel(at, last, start_ref, normed_ref, decoder_ref, decoder_bias_ref, *refs):
    if last:
        out_ref, pooled = refs
    else:
        far_ref, out_ref, next_ref, pooled, sem = refs
    queries, chunk = pooled.shape
    rows = normed_ref.shape[0] * GROUP // queries
    if not last:
        copy = pltpu.make_async_copy(far_ref.at[:, pl.ds((at + 1) * chunk, chunk)], next_ref, sem)
        copy.start()

    @pl.when(start_ref[0] >= 0)
    def _():
        for group in range(queries // GROUP):
            part = normed_ref[group * rows : (group + 1) * rows, :]
            pool(part, decoder_ref, decoder_bias_ref[at], group, rows // GROUP, pooled)
        out_ref[...] = keep_vocab(start_ref[0] + at * chunk, pooled)

    if not last:
        copy.wait()


def slot_queries(cand, base, tile_total):
    depth, queries = cand.shape
    row = lax.broadcasted_iota(jnp.int32, (tile_total, queries), 0) + base
    hits = jnp.zeros((tile_total, queries), F32)
    for place in range(depth):
        hits = jnp.where(cand[place : place + 1, :] == row, 1.0, hits)
    hits = hits.astype(BF16)
    mine = lax.broadcasted_iota(jnp.int32, (queries, queries), 0)
    other = lax.broadcasted_iota(jnp.int32, (queries, queries), 1)
    last = (((1,), (1,)), ((), ()))
    turned = lax.dot_general(
        jnp.where(mine == other, 1.0, 0.0).astype(BF16), hits, last, preferred_element_type=F32
    )
    before = lax.dot_general(
        jnp.where(other < mine, 1.0, 0.0).astype(BF16), hits, last, preferred_element_type=F32
    )
    rank = jnp.where(turned > 0.0, before, -1.0).astype(BF16)
    slots = tile_total * MOST
    tile = lax.broadcasted_iota(jnp.int32, (tile_total, slots), 0)
    spread = jnp.where(lax.broadcasted_iota(jnp.int32, (tile_total, slots), 1) // MOST == tile, 1.0, 0.0)
    wide = jnp.dot(rank, spread.astype(BF16), preferred_element_type=F32)
    want = (lax.broadcasted_iota(jnp.int32, (queries, slots), 1) % MOST).astype(F32)
    query = lax.broadcasted_iota(jnp.int32, (queries, slots), 0)
    return jnp.sum(jnp.where(wide == want, query, 0), axis=0, keepdims=True)


def score_kernel(at, last, parties, depth, place_ref, occupancy_ref, *refs):
    refs = list(refs)
    docs_ref = refs.pop(0) if at else None
    far_ref = None if last else refs.pop(0)
    weight_refs, refs = refs[:parties], refs[parties:]
    before_ref = refs.pop(0) if at else None
    if last:
        slots_ref, out_ref, turned, total = refs
    elif at:
        after_ref, next_ref, turned, sems = refs
    else:
        after_ref, next_ref, slots_ref, turned, sems, docs_ref, own_sems = refs
    tile_total, blocks, docs, terms = docs_ref.shape
    tiles = LANES // MOST
    steps = tile_total // tiles
    chunk = blocks * terms
    queries = weight_refs[0].shape[0]
    rows = tiles * docs
    always = place_ref[0] >= 0

    def fetch(part, target, signals):
        return [
            pltpu.make_async_copy(far_ref.at[tile, pl.ds(part * blocks, blocks)], target.at[tile], signals.at[tile])
            for tile in range(tile_total)
        ]

    own = [] if at else fetch(0, docs_ref, own_sems)
    later = [] if last else fetch(at + 1, next_ref, sems)
    queue = own + later

    def start(number):
        for copy in queue[:number]:
            copy.start()
        del queue[:number]

    start(2 * tiles if own else len(queue))

    @pl.when(always)
    def _():
        for party, ref in enumerate(weight_refs):
            turned[party * queries : (party + 1) * queries, :] = ref[:, :chunk]
            if not at:
                cand = ref[:depth, chunk : chunk + queries].astype(F32).astype(jnp.int32)
                found = slot_queries(cand, place_ref[0] * tile_total, tile_total)
                slots_ref[party : party + 1, :] = found + party * queries % LANES

    def work(step):
        left = [
            jnp.concatenate(
                [
                    jnp.where(
                        occupancy_ref[tile, at * blocks + block] != 0, docs_ref[tile, block], 0.0
                    ).astype(BF16)
                    for block in range(blocks)
                ],
                axis=1,
            )
            for tile in range(step * tiles, (step + 1) * tiles)
        ]
        value = lax.dot_general(
            jnp.concatenate(left, axis=0),
            turned[...],
            (((1,), (1,)), ((), ())),
            preferred_element_type=F32,
        )
        if at:
            value = value + before_ref[step * rows : (step + 1) * rows, :]
        if not last:
            after_ref[step * rows : (step + 1) * rows, :] = value
            return
        lane = lax.broadcasted_iota(jnp.int32, (docs, LANES), 1) // MOST
        term_count, share = total.shape[1], docs // total.shape[1]
        for party in range(parties):
            begin = party * queries // LANES * LANES
            source = slots_ref[party : party + 1, step * LANES : (step + 1) * LANES]
            source = jnp.broadcast_to(source, (docs, LANES))
            part = None
            for tile in range(tiles):
                held = value[tile * docs : (tile + 1) * docs, begin : begin + LANES]
                held = jnp.take_along_axis(held, source, axis=1, mode="promise_in_bounds")
                part = held if part is None else jnp.where(lane == tile, held, part)
            for term in range(term_count):
                total[party, term, step * share : (step + 1) * share, :] = part[term * share : (term + 1) * share]

    if own:
        for step in range(steps):
            for copy in own[step * tiles : (step + 1) * tiles]:
                copy.wait()
            start(2 * tiles)

            @pl.when(always)
            def _(step=step):
                work(step)
    else:

        @pl.when(always)
        def _():
            for step in range(steps):
                work(step)
            if last:
                for party in range(parties):
                    out_ref[place_ref[0] ^ party] = total[party].astype(BF16)

    start(len(queue))
    for copy in later:
        copy.wait()


def ranks(cand, row, queries):
    depth, total = cand.shape
    hits = jnp.zeros((row.shape[0], total), F32)
    for place in range(depth):
        hits = jnp.where(cand[place : place + 1, :] == row, 1.0, hits)
    earlier = lax.broadcasted_iota(jnp.int32, (total, total), 0)
    later = lax.broadcasted_iota(jnp.int32, (total, total), 1)
    before = jnp.dot(
        hits.astype(BF16), jnp.where(earlier < later, 1.0, 0.0).astype(BF16), preferred_element_type=F32
    )
    return jnp.where(hits > 0.0, before, -1.0)


def final_kernel(cand_ref, got_ref, out_ref):
    docs_n, term_count, rows, _ = got_ref.shape
    depth, share, queries = out_ref.shape
    groups = rows // share
    tiles = LANES // MOST
    all_tiles = docs_n * groups * tiles
    cand = cand_ref[...]
    rank = ranks(cand, lax.broadcasted_iota(jnp.int32, (all_tiles, queries), 0), queries)
    slot = lax.broadcasted_iota(jnp.int32, (LANES, tiles * queries), 0)
    twice = jnp.concatenate([cand, cand], axis=1)
    lane = lax.broadcasted_iota(jnp.int32, (1, 2 * queries), 1) // queries
    result = [jnp.zeros((share, 2 * queries), F32) for _ in range(depth)]
    for doc in range(docs_n):
        summed = got_ref[doc, 0].astype(F32)
        for term in range(1, term_count):
            summed = summed + got_ref[doc, term].astype(F32)
        for group in range(groups):
            first = (doc * groups + group) * tiles
            want = jnp.concatenate(
                [
                    jnp.where(rank[first + k : first + k + 1] >= 0.0, rank[first + k : first + k + 1] + k * MOST, -1.0)
                    for k in range(tiles)
                ],
                axis=1,
            ).astype(jnp.int32)
            hot = jnp.where(slot == want, 1.0, 0.0).astype(BF16)
            value = summed[group * share : (group + 1) * share]
            high = value.astype(BF16)
            low = (value - high.astype(F32)).astype(BF16)
            moved = jnp.dot(high, hot, preferred_element_type=F32) + jnp.dot(
                low, hot, preferred_element_type=F32
            )
            for pair in range(tiles // 2):
                held = moved[:, pair * 2 * queries : (pair + 1) * 2 * queries]
                name = first + pair * 2 + lane
                for place in range(depth):
                    result[place] = jnp.where(twice[place : place + 1] == name, held, result[place])
    for place in range(depth):
        out_ref[place] = result[place][:, :queries] + result[place][:, queries:]


def body(
    query_states,
    token_ids,
    transform_weight,
    transform_bias,
    norm_gain,
    norm_bias,
    decoder_weight,
    decoder_bias,
    candidates,
    occupancy,
    doc_blocks,
):
    query_count, length, width = query_states.shape
    vocab = decoder_weight.shape[1]
    tile_local, blocks, docs, terms = doc_blocks.shape
    depth = candidates.shape[1]
    term_index, doc_index = lax.axis_index("term"), lax.axis_index("doc")
    doc_count, term_count = lax.axis_size("doc"), lax.axis_size("term")
    share = docs // term_count
    all_queries = doc_count * query_count
    tiles = LANES // MOST
    steps = tile_local // tiles
    chunks = 3
    chunk = vocab // chunks
    few = blocks // chunks
    cand = candidates.T
    start = (term_index * vocab).reshape(1)
    place = doc_index.reshape(1)
    rows = query_count * length
    far, near = pltpu.HBM, pltpu.VMEM

    def put(space, *operands):
        return [pltpu.with_memory_space_constraint(operand, space) for operand in operands]

    def call(name, kernel, in_specs, out_shape, scratch, macs, limit, operands):
        return pl.pallas_call(
            kernel,
            in_specs=in_specs,
            out_specs=jax.tree.map(lambda _: WHOLE, out_shape),
            out_shape=out_shape,
            scratch_shapes=scratch,
            cost_estimate=pl.CostEstimate(flops=2 * macs, bytes_accessed=10**6, transcendentals=0),
            compiler_params=pltpu.CompilerParams(vmem_limit_bytes=limit),
            name=name,
        )(*operands)

    next_decoder = near((width, chunk), BF16)
    next_docs = near((tile_local, few, docs, terms), BF16)
    pooled = pltpu.VMEM((query_count, chunk), F32)
    piece, normed, first_decoder, all_bias = call(
        "expand_first",
        first_kernel,
        [SCALARS] + [FAR] * 9,
        [
            jax.ShapeDtypeStruct((query_count, chunk + LANES), BF16),
            near((rows, width), BF16),
            next_decoder,
            near((chunks, 1, chunk), F32),
        ],
        [
            pltpu.VMEM(query_states.shape, BF16),
            pltpu.VMEM(transform_weight.shape, BF16),
            pltpu.VMEM((width, chunk), BF16),
            pltpu.VMEM((1, width), F32),
            pltpu.VMEM((1, width), F32),
            pltpu.VMEM((1, width), F32),
            pltpu.VMEM((length, query_count), jnp.int32),
            pltpu.VMEM(cand.shape, jnp.int32),
            pltpu.VMEM((GROUP * length, query_count), F32),
            pooled,
            pltpu.SemaphoreType.DMA((10 + chunks,)),
        ],
        rows * width * (width + chunk),
        13 << 20,
        [start]
        + put(
            far,
            query_states,
            token_ids.T,
            transform_weight,
            transform_bias,
            norm_gain,
            norm_bias,
            decoder_weight,
            decoder_bias,
            cand,
        ),
    )
    own, decoder = [piece], [first_decoder]
    for at in range(1, chunks):
        final = at == chunks - 1
        piece, *decoder = call(
            "expand_next",
            functools.partial(chunk_kernel, at, final),
            [SCALARS] + [WHOLE] * 3 + ([] if final else [FAR]),
            [jax.ShapeDtypeStruct((query_count, chunk), BF16)] + ([] if final else [next_decoder]),
            [pooled] + ([] if final else [pltpu.SemaphoreType.DMA(())]),
            rows * width * chunk,
            6 << 20,
            [start, *put(near, normed, *decoder, all_bias), *([] if final else put(far, decoder_weight))],
        )
        own.append(piece)

    partial_scores, slots = None, None
    for at in range(chunks):
        held = [own[at]] + [None] * (doc_count - 1)
        bit, known = doc_count // 2, [0]
        while bit:
            swap = [(i, i ^ bit) for i in range(doc_count)]
            for k in list(known):
                held[k | bit] = lax.ppermute(held[k], "doc", swap)
                known.append(k | bit)
            if at >= 2 and bit == doc_count // 2:
                held[bit], partial_scores = lax.optimization_barrier((held[bit], partial_scores))
            bit //= 2
        last = at == chunks - 1
        if last:
            out_shape = [jax.ShapeDtypeStruct((doc_count, term_count, steps * share, LANES), BF16)]
            scratch = [pltpu.VMEM((doc_count, term_count, steps * share, LANES), F32)]
        else:
            out_shape = [near((tile_local * docs, all_queries), F32), next_docs]
            if at == 0:
                out_shape.append(near((doc_count, tile_local * MOST), jnp.int32))
            scratch = [pltpu.SemaphoreType.DMA((tile_local,))]
            if at == 0:
                scratch += [
                    pltpu.VMEM((tile_local, few, docs, terms), BF16),
                    pltpu.SemaphoreType.DMA((tile_local,)),
                ]
        operands = [place, occupancy, *(put(near, near_docs) if at else [])]
        in_specs = [SCALARS, SCALARS] + [WHOLE] * min(at, 1)
        if not last:
            operands += put(far, doc_blocks)
            in_specs.append(FAR)
        extra = ([partial_scores] if at else []) + ([slots] if last else [])
        operands += held + put(near, *extra)
        in_specs += [WHOLE] * (doc_count + len(extra))
        results = call(
            "score_last" if last else "score_chunk",
            functools.partial(score_kernel, at, last, doc_count, depth),
            in_specs,
            out_shape,
            [pltpu.VMEM((all_queries, chunk), BF16)] + scratch,
            4 * tile_local * docs * chunk * all_queries,
            (8 if at else 14) << 20,
            operands,
        )
        if last:
            sent = results[0]
        else:
            partial_scores, near_docs = results[:2]
            slots = results[2] if at == 0 else slots
    weights = jnp.concatenate([own[0][:, :chunk], *own[1:]], axis=1)

    everyone = doc_count * term_count
    got = lax.all_to_all(
        sent.reshape(everyone, steps * share, LANES), ("doc", "term"), split_axis=0, concat_axis=0, tiled=True
    ).reshape(doc_count, term_count, steps * share, LANES)
    scores = call(
        "place",
        final_kernel,
        [WHOLE, WHOLE],
        jax.ShapeDtypeStruct((depth, share, query_count), F32),
        [],
        10**6,
        8 << 20,
        [cand, got],
    )
    return weights, scores.transpose(2, 0, 1)


def solution(mesh):
    placed = (
        P("doc", None, None),
        P("doc", None),
        P(),
        P(),
        P(),
        P(),
        P(None, "term"),
        P("term"),
        P("doc", None),
        P("doc", "term"),
        P("doc", "term", None, None),
    )
    return jax.shard_map(
        body,
        mesh=mesh,
        in_specs=placed,
        out_specs=(P("doc", "term"), P("doc", None, "term")),
        check_vma=False,
    )
```

time: 83.7 us -> 65.3 us (0.78)
  local copies, waits for them, and re-layouts: 15.6 us -> 0.02 us
  waiting for transfers between devices: 23.8 us -> 17.9 us
  starting transfers between devices: 8.65 us -> 11.1 us
    unnamed x16 -> x4, local copies, waits for them, and re-layouts: 12.7 us -> 0.01 us
    ppermute x6 -> x9, waiting for transfers between devices: 8.27 us -> 2.38 us  [body(): held[k | bit] = lax.ppermute(held[k], 'doc', swap)]
    reshape x4 -> x0, local copies, waits for them, and re-layouts: 2.8 us -> none  [the longest x1 0.73 us: body(): decoder_bias.reshape(1, -1)]
    ppermute x6 -> x9, starting transfers between devices: 3.72 us -> 5.5 us  [body(): held[k | bit] = lax.ppermute(held[k], 'doc', swap)]
    pallas_call x4 -> x7, Pallas kernels: 33.5 us -> 34.3 us  [call(): pl.pallas_call(kernel, in_specs=in_specs, out_specs=jax.tree.map(lambda _...]
  transfers between devices with their start and end apart: 7 -> 10, of which waited for: 3 -> 4; matrix products, arithmetic and copies ran while one was open for 1% -> 1% of each run, Pallas kernels for 13% -> 27%
where the time goes in v2:
time: 65.3 us; the launch traced here: 64.9 us
  Pallas kernels  34.3 us (53%)
  waiting for transfers between devices  17.9 us (27%)
  starting transfers between devices  11.1 us (17%)
  other arithmetic  0.81 us (1%)
  between operations  0.74 us (1%)
    pallas_call x7, Pallas kernels, call(): pl.pallas_call(kernel, in_specs=in_specs, out_specs=jax.tree.map(lambda _...  34.3 us
    all_to_all x1, waiting for transfers between devices, body(): lax.all_to_all(sent.reshape(everyone, steps * share, LANES), ('doc', 'ter...  15.5 us
    all_to_all x1, starting transfers between devices, body(): lax.all_to_all(sent.reshape(everyone, steps * share, LANES), ('doc', 'ter...  5.61 us
    ppermute x9, starting transfers between devices, body(): held[k | bit] = lax.ppermute(held[k], 'doc', swap)  5.5 us
    ppermute x9, waiting for transfers between devices, body(): held[k | bit] = lax.ppermute(held[k], 'doc', swap)  2.38 us
  transfers between devices with their start and end apart: 10, of which 4 were waited for; matrix products, arithmetic and copies ran while one was open for 1% of the time, Pallas kernels for 27%

profile of v2, /device:TPU:0, one launch (start us, length us, event | category | flops | bytes accessed | tf_op | source)
XLA Modules:
  0.0 64.9 jit_solution(4260054527982742849)
XLA Ops:
  0.6 10.9 %expand_first.1 = (bf16[64,1408]{1,0:T(8,128)(2,1)S(1)}, bf16[2048,768]{1,0:T(8,128)(2,1)S(1)}, bf16[768,1280]{1,0:T(8,128)(2,1)S(1)}, f32[3,1,1280]{2,1,0:T(1,128)S(1)}) custom-call(s32[1]{0:T(128)} %bitcast.start_ref, bf16[64,32,768]{2,1,0:T(8,128)(2,1)} %states_hbm.1, s32[32,64]{1,0:T(8,128)} %bitcast.11, bf16[768,768]{1,0:T(8,128)(2,1)} %transform_hbm.1, ...), custom_call_target="tpu_custom_call" | custom-call | flops 6442450944 | bytes 1000000 | tf_op jit(solution)/shard_map/expand_first/pallas_call | solution.py:410
  11.5 0.5 collective-permute-start
  12.0 2.6 %collective-permute-start.1 = (bf16[64,1408]{1,0:T(8,128)(2,1)S(1)}, bf16[64,1408]{1,0:T(8,128)(2,1)S(1)}, u32[]{:S(2)}, u32[]{:S(2)}) collective-permute-start(bf16[64,1408]{1,0:T(8,128)(2,1)S(1)} %get-tuple-element.15.refs_1_), channel_id=1, source_target_pairs={{0,16},{8,24},{16,0},{24,8},{1,17},{9,25},{17,1},{25,9},{2,18},{10... | collective-permute-start | bytes 540680 | tf_op jit(solution)/shard_map/ppermute | solution.py:485
  14.6 4.3 %expand_next.2 = (bf16[64,1280]{1,0:T(8,128)(2,1)S(1)}, bf16[768,1280]{1,0:T(8,128)(2,1)S(1)}) custom-call(s32[1]{0:T(128)} %bitcast.start_ref, bf16[2048,768]{1,0:T(8,128)(2,1)S(1)} %get-tuple-element.16.normed_ref, bf16[768,1280]{1,0:T(8,128)(2,1)S(1)} %get-tuple-element.17.decoder_ref, f32[3,1,1280]{2,1,0:T(1,128)S(1)} %get-tuple-element.18.decoder_bias_ref, ...), custom_call_target="tpu_custom_call" | custom-call | flops 4026531840 | bytes 1000000 | tf_op jit(solution)/shard_map/expand_next/pallas_call | solution.py:410
  18.9 0.2 collective-permute-start.3
  19.1 0.3 collective-permute-start.4
  19.4 0.4 collective-permute-done.1.refs_3_
  19.8 0.0 collective-permute-start.2
  19.8 0.0 copy-start.1
  19.8 4.3 %expand_next.3.refs_1_ = bf16[64,1280]{1,0:T(8,128)(2,1)S(1)} custom-call(s32[1]{0:T(128)} %bitcast.start_ref, bf16[2048,768]{1,0:T(8,128)(2,1)S(1)} %get-tuple-element.16.normed_ref, bf16[768,1280]{1,0:T(8,128)(2,1)S(1)} %get-tuple-element.20.decoder_ref, f32[3,1,1280]{2,1,0:T(1,128)S(1)} %get-tuple-element.18.decoder_bias_ref), custom_call_target="tpu_custom_call" | custom-call | flops 4026531840 | bytes 1000000 | tf_op jit(solution)/shard_map/expand_next/pallas_call | solution.py:410
  24.0 0.6 collective-permute-start.6
  24.6 1.0 %collective-permute-done.4.refs_4_ = bf16[64,1280]{1,0:T(8,128)(2,1)S(1)} collective-permute-done((bf16[64,1280]{1,0:T(8,128)(2,1)S(1)}, bf16[64,1280]{1,0:T(8,128)(2,1)S(1)}, u32[]{:S(2)}, u32[]{:S(2)}) %collective-permute-start.4) | collective-permute-done | bytes 163872 | tf_op jit(solution)/shard_map/ppermute | solution.py:485
  25.6 0.8 %collective-permute-start.7 = (bf16[64,1280]{1,0:T(8,128)(2,1)S(1)}, bf16[64,1280]{1,0:T(8,128)(2,1)S(1)}, u32[]{:S(2)}, u32[]{:S(2)}) collective-permute-start(bf16[64,1280]{1,0:T(8,128)(2,1)S(1)} %expand_next.3.refs_1_), channel_id=1, source_target_pairs={{0,16},{8,24},{16,0},{24,8},{1,17},{9,25},{17,1},{25,9},{2,18},{10... | collective-permute-start | bytes 491528 | tf_op jit(solution)/shard_map/ppermute | solution.py:485
  26.4 0.0 collective-permute-done.refs_2_
  26.4 0.0 collective-permute-start.5
  26.4 0.0 collective-permute-done.2.refs_4_
  26.4 0.0 copy-done.1
  26.4 5.7 %score_chunk.2 = (f32[2048,256]{1,0:T(8,128)S(1)}, bf16[16,10,128,128]{3,2,1,0:T(8,128)(2,1)S(1)}, s32[4,512]{1,0:T(4,128)S(1)}) custom-call(s32[1]{0:T(128)} %bitcast.3.place_ref, s32[16,30]{1,0:T(8,128)S(1)} %copy-done.1, bf16[16,30,128,128]{3,2,1,0:T(8,128)(2,1)} %refs_1_.1, bf16[64,1408]{1,0:T(8,128)(2,1)S(1)} %get-tuple-element.15.refs_1_, ...), custom_call_target="tpu_custom_call" | custom-call | flops 5368709120 | bytes 1000000 | tf_op jit(solution)/shard_map/score_chunk/pallas_call | solution.py:410
  32.0 0.0 collective-permute-done.3.refs_3_
  32.1 0.0 collective-permute-done.5.refs_5_
  32.1 3.3 %score_chunk.3 = (f32[2048,256]{1,0:T(8,128)S(1)}, bf16[16,10,128,128]{3,2,1,0:T(8,128)(2,1)S(1)}) custom-call(s32[1]{0:T(128)} %bitcast.3.place_ref, s32[16,30]{1,0:T(8,128)S(1)} %copy-done.1, bf16[16,10,128,128]{3,2,1,0:T(8,128)(2,1)S(1)} %get-tuple-element.21.refs_0_, bf16[16,30,128,128]{3,2,1,0:T(8,128)(2,1)} %refs_1_.1, ...), custom_call_target="tpu_custom_call" | custom-call | flops 5368709120 | bytes 1000000 | tf_op jit(solution)/shard_map/score_chunk/pallas_call | solution.py:410
  35.3 0.0 collective-permute-done.7.refs_3_
  35.4 0.6 collective-permute-start.8
  35.9 0.0 collective-permute-done.6.refs_2_
  35.9 1.0 %collective-permute-done.8.refs_4_ = bf16[64,1280]{1,0:T(8,128)(2,1)S(1)} collective-permute-done((bf16[64,1280]{1,0:T(8,128)(2,1)S(1)}, bf16[64,1280]{1,0:T(8,128)(2,1)S(1)}, u32[]{:S(2)}, u32[]{:S(2)}) %collective-permute-start.8) | collective-permute-done | bytes 163872 | tf_op jit(solution)/shard_map/ppermute | solution.py:485
  36.9 0.0 copy-start
  36.9 3.8 %score_last.1 = bf16[4,8,64,128]{3,2,1,0:T(8,128)(2,1)} custom-call(s32[1]{0:T(128)} %bitcast.3.place_ref, s32[16,30]{1,0:T(8,128)S(1)} %copy-done.1, bf16[16,10,128,128]{3,2,1,0:T(8,128)(2,1)S(1)} %get-tuple-element.23.refs_0_, bf16[64,1280]{1,0:T(8,128)(2,1)S(1)} %expand_next.3.refs_1_, bf16[64,1280]{1,0:T(8,128)(2,1)S(1)} %collective-permute-done.6.refs_2_, ...), custom_call_target="tpu_custom_call" | custom-call | flops 5368709120 | bytes 1000000 | tf_op jit(solution)/shard_map/score_last/pallas_call | solution.py:410
  40.7 5.6 %all-to-all-start = ((bf16[32,64,128]{2,1,0:T(8,128)(2,1)}), bf16[32,64,128]{2,1,0:T(8,128)(2,1)S(1)}, u32[]{:S(2)}, u32[]{:S(2)}) async-start(bf16[32,64,128]{2,1,0:T(8,128)(2,1)} %bitcast.4), calls=%async_computation | async-start | bytes 1048576 | tf_op jit(solution)/shard_map/all_to_all | solution.py:530
  46.4 0.8 %pad_maximum_fusion = bf16[64,3840]{1,0:T(8,128)(2,1)} fusion(bf16[64,1280]{1,0:T(8,128)(2,1)S(1)} %expand_next.3.refs_1_, bf16[64,1280]{1,0:T(8,128)(2,1)S(1)} %get-tuple-element.19.refs_2_, bf16[64,1280]{1,0:T(8,128)(2,1)S(1)} %slice.3), kind=kLoop, calls=%fused_computation | loop fusion | flops 1474560 | bytes 983040 | tf_op jit(solution)/shard_map/concatenate | solution.py:527
  47.2 15.5 %all-to-all-done = bf16[32,64,128]{2,1,0:T(8,128)(2,1)S(1)} async-done(((bf16[32,64,128]{2,1,0:T(8,128)(2,1)}), bf16[32,64,128]{2,1,0:T(8,128)(2,1)S(1)}, u32[]{:S(2)}, u32[]{:S(2)}) %all-to-all-start) | async-done | bytes 524320 | tf_op jit(solution)/shard_map/all_to_all | solution.py:530
  62.7 0.0 copy-done
  62.7 2.2 %place.1 = f32[32,16,64]{2,1,0:T(8,128)} custom-call(s32[32,64]{1,0:T(8,128)S(1)} %bitcast.9, bf16[4,8,64,128]{3,2,1,0:T(8,128)(2,1)S(1)} %bitcast.7), custom_call_target="tpu_custom_call" | custom-call | flops 2000000 | bytes 1000000 | tf_op jit(solution)/shard_map/place/pallas_call | solution.py:410
  (1 shorter events, 0.0 us)
Async XLA Ops:
  11.5 14.8 %collective-permute-start = (bf16[64,1408]{1,0:T(8,128)(2,1)S(1)}, bf16[64,1408]{1,0:T(8,128)(2,1)S(1)}, u32[]{:S(2)}, u32[]{:S(2)}) collective-permute-start(bf16[64,1408]{1,0:T(8,128)(2,1)S(1)} %get-tuple-element.15.refs_1_), channel_id=1, source_target_pairs={{0,8},{8,0},{16,24},{24,16},{1,9},{9,1},{17,25},{25,17},{2,10},{10... | collective-permute-start | bytes 540680 | tf_op jit(solution)/shard_map/ppermute | solution.py:485
  12.0 7.7 %collective-permute-start.1 = (bf16[64,1408]{1,0:T(8,128)(2,1)S(1)}, bf16[64,1408]{1,0:T(8,128)(2,1)S(1)}, u32[]{:S(2)}, u32[]{:S(2)}) collective-permute-start(bf16[64,1408]{1,0:T(8,128)(2,1)S(1)} %get-tuple-element.15.refs_1_), channel_id=1, source_target_pairs={{0,16},{8,24},{16,0},{24,8},{1,17},{9,25},{17,1},{25,9},{2,18},{10... | collective-permute-start | bytes 540680 | tf_op jit(solution)/shard_map/ppermute | solution.py:485
  18.9 13.2 %collective-permute-start.3 = (bf16[64,1280]{1,0:T(8,128)(2,1)S(1)}, bf16[64,1280]{1,0:T(8,128)(2,1)S(1)}, u32[]{:S(2)}, u32[]{:S(2)}) collective-permute-start(bf16[64,1280]{1,0:T(8,128)(2,1)S(1)} %get-tuple-element.19.refs_2_), channel_id=1, source_target_pairs={{0,8},{8,0},{16,24},{24,16},{1,9},{9,1},{17,25},{25,17},{2,10},{10... | collective-permute-start | bytes 491528 | tf_op jit(solution)/shard_map/ppermute | solution.py:485
  19.1 6.4 %collective-permute-start.4 = (bf16[64,1280]{1,0:T(8,128)(2,1)S(1)}, bf16[64,1280]{1,0:T(8,128)(2,1)S(1)}, u32[]{:S(2)}, u32[]{:S(2)}) collective-permute-start(bf16[64,1280]{1,0:T(8,128)(2,1)S(1)} %get-tuple-element.19.refs_2_), channel_id=1, source_target_pairs={{0,16},{8,24},{16,0},{24,8},{1,17},{9,25},{17,1},{25,9},{2,18},{10... | collective-permute-start | bytes 491528 | tf_op jit(solution)/shard_map/ppermute | solution.py:485
  19.8 6.6 %collective-permute-start.2 = (bf16[64,1408]{1,0:T(8,128)(2,1)S(1)}, bf16[64,1408]{1,0:T(8,128)(2,1)S(1)}, u32[]{:S(2)}, u32[]{:S(2)}) collective-permute-start(bf16[64,1408]{1,0:T(8,128)(2,1)S(1)} %collective-permute-done.1.refs_3_), channel_id=1, source_target_pairs={{0,8},{8,0},{16,24},{24,16},{1,9},{9,1},{17,25},{25,17},{2,10},{10... | collective-permute-start | bytes 540680 | tf_op jit(solution)/shard_map/ppermute | solution.py:485
  19.8 6.6 %copy-start.1 = (s32[16,30]{1,0:T(8,128)S(1)}, s32[16,30]{1,0:T(8,128)}, u32[]{:S(2)}) copy-start(s32[16,30]{1,0:T(8,128)} %occupancy_ref.5) | copy-start | bytes 5764
  24.0 11.9 %collective-permute-start.6 = (bf16[64,1280]{1,0:T(8,128)(2,1)S(1)}, bf16[64,1280]{1,0:T(8,128)(2,1)S(1)}, u32[]{:S(2)}, u32[]{:S(2)}) collective-permute-start(bf16[64,1280]{1,0:T(8,128)(2,1)S(1)} %expand_next.3.refs_1_), channel_id=1, source_target_pairs={{0,8},{8,0},{16,24},{24,16},{1,9},{9,1},{17,25},{25,17},{2,10},{10... | collective-permute-start | bytes 491528 | tf_op jit(solution)/shard_map/ppermute | solution.py:485
  25.6 9.8 %collective-permute-start.7 = (bf16[64,1280]{1,0:T(8,128)(2,1)S(1)}, bf16[64,1280]{1,0:T(8,128)(2,1)S(1)}, u32[]{:S(2)}, u32[]{:S(2)}) collective-permute-start(bf16[64,1280]{1,0:T(8,128)(2,1)S(1)} %expand_next.3.refs_1_), channel_id=1, source_target_pairs={{0,16},{8,24},{16,0},{24,8},{1,17},{9,25},{17,1},{25,9},{2,18},{10... | collective-permute-start | bytes 491528 | tf_op jit(solution)/shard_map/ppermute | solution.py:485
  26.4 5.7 %collective-permute-start.5 = (bf16[64,1280]{1,0:T(8,128)(2,1)S(1)}, bf16[64,1280]{1,0:T(8,128)(2,1)S(1)}, u32[]{:S(2)}, u32[]{:S(2)}) collective-permute-start(bf16[64,1280]{1,0:T(8,128)(2,1)S(1)} %collective-permute-done.4.refs_4_), channel_id=1, source_target_pairs={{0,8},{8,0},{16,24},{24,16},{1,9},{9,1},{17,25},{25,17},{2,10},{10... | collective-permute-start | bytes 491528 | tf_op jit(solution)/shard_map/ppermute | solution.py:485
  35.4 1.6 %collective-permute-start.8 = (bf16[64,1280]{1,0:T(8,128)(2,1)S(1)}, bf16[64,1280]{1,0:T(8,128)(2,1)S(1)}, u32[]{:S(2)}, u32[]{:S(2)}) collective-permute-start(bf16[64,1280]{1,0:T(8,128)(2,1)S(1)} %collective-permute-done.7.refs_3_), channel_id=1, source_target_pairs={{0,8},{8,0},{16,24},{24,16},{1,9},{9,1},{17,25},{25,17},{2,10},{10... | collective-permute-start | bytes 491528 | tf_op jit(solution)/shard_map/ppermute | solution.py:485
  36.9 25.8 %copy-start = (s32[64,32]{0,1:T(8,128)S(1)}, s32[64,32]{0,1:T(8,128)}, u32[]{:S(2)}) copy-start(s32[64,32]{0,1:T(8,128)} %param.19) | copy-start | bytes 24580
  40.7 22.0 %all-to-all-start = ((bf16[32,64,128]{2,1,0:T(8,128)(2,1)}), bf16[32,64,128]{2,1,0:T(8,128)(2,1)S(1)}, u32[]{:S(2)}, u32[]{:S(2)}) async-start(bf16[32,64,128]{2,1,0:T(8,128)(2,1)} %bitcast.4), calls=%async_computation | async-start | bytes 1048576 | tf_op jit(solution)/shard_map/all_to_all | solution.py:530

commit v3 on v2

v3 whole, which is shorter than its diff:
```python
import functools
import math

import jax
import jax.numpy as jnp
from jax import lax
from jax.experimental import pallas as pl
from jax.experimental.pallas import tpu as pltpu
from jax.sharding import PartitionSpec as P

VOCAB = 30522
MOST = 32
LANES = 128
GROUP = 8
F32 = jnp.float32
BF16 = jnp.bfloat16
WHOLE = pl.BlockSpec(memory_space=pltpu.VMEM)
FAR = pl.BlockSpec(memory_space=pltpu.HBM)
SCALARS = pl.BlockSpec(memory_space=pltpu.SMEM)


def gelu(value):
    return 0.5 * value * (1.0 + lax.erf(value * math.sqrt(0.5)))


def normed_rows(states, live_at, first, transform, bias, gain, shift):
    queries, length, width = states.shape
    rows = queries * length
    row = lax.broadcasted_iota(jnp.int32, live_at.shape, 0)
    lane = lax.broadcasted_iota(jnp.int32, live_at.shape, 1)
    own = jnp.where(lane == first + row % queries, live_at, 0.0)
    live = jnp.sum(own, axis=1, keepdims=True) > 0.0
    row = lax.broadcasted_iota(jnp.int32, (rows, 1), 0)
    source = row % queries * length + jnp.where(live, row // queries, 0)
    column = lax.broadcasted_iota(jnp.int32, (rows, rows), 1)
    order = jnp.where(column == source, 1.0, 0.0).astype(BF16)
    moved = jnp.dot(order, states.reshape(rows, width), preferred_element_type=F32)
    hidden = jnp.dot(moved.astype(BF16), transform, preferred_element_type=F32)
    hidden = gelu(hidden + bias)
    centred = hidden - jnp.mean(hidden, axis=1, keepdims=True)
    spread = jnp.mean(centred * centred, axis=1, keepdims=True)
    return (centred * lax.rsqrt(spread + 1e-06) * gain + shift).astype(BF16)


def place_of(rows, live_at, tokens_ref):
    length = tokens_ref.shape[0]
    at = lax.broadcasted_iota(jnp.int32, (rows, length), 0) // GROUP
    spot = lax.broadcasted_iota(jnp.int32, (rows, length), 1)
    pick = jnp.where(at == spot, 1.0, 0.0).astype(BF16)
    alive = jnp.where(tokens_ref[...] != 0, 1.0, 0.0).astype(BF16)
    live_at[...] = jnp.dot(pick, alive, preferred_element_type=F32)


def pool(rows, decoder_ref, bias, group, length, out_ref):
    logits = jnp.dot(rows, decoder_ref[...], preferred_element_type=F32)
    top = jnp.max(logits.reshape(length, GROUP, logits.shape[1]), axis=0)
    out_ref[group * GROUP : (group + 1) * GROUP, :] = jnp.log1p(
        jnp.maximum(top + bias, 0.0)
    )


def keep_vocab(start, pooled):
    column = start + lax.broadcasted_iota(jnp.int32, pooled.shape, 1)
    return jnp.where(column < VOCAB, pooled[...], 0.0).astype(BF16)


def first_kernel(
    start_ref,
    states_hbm,
    tokens_hbm,
    transform_hbm,
    bias_hbm,
    gain_hbm,
    shift_hbm,
    decoder_hbm,
    decoder_bias_hbm,
    cand_hbm,
    out_ref,
    normed_ref,
    next_ref,
    decoder_bias_ref,
    states_ref,
    transform_ref,
    decoder_ref,
    bias_ref,
    gain_ref,
    shift_ref,
    tokens_ref,
    cand_ref,
    live_at,
    pooled,
    sems,
):
    queries, length, _ = states_ref.shape
    groups = queries // GROUP
    rows = GROUP * length
    chunk = decoder_ref.shape[1]
    always = start_ref[0] >= 0
    copies = []

    def bring(source, target):
        copy = pltpu.make_async_copy(source, target, sems.at[len(copies)])
        copies.append(copy)
        copy.start()

    half = pl.ds(0, GROUP)
    other = pl.ds(GROUP, queries - GROUP)
    bring(tokens_hbm, tokens_ref)
    bring(bias_hbm, bias_ref.at[0])
    bring(gain_hbm, gain_ref.at[0])
    bring(shift_hbm, shift_ref.at[0])
    bring(states_hbm.at[half], states_ref.at[half])
    bring(transform_hbm, transform_ref)
    early = len(copies)
    bring(decoder_hbm.at[:, pl.ds(0, chunk)], decoder_ref)
    bring(decoder_bias_hbm, decoder_bias_ref.at[0])
    bring(states_hbm.at[other], states_ref.at[other])
    bring(cand_hbm, cand_ref)
    middle = len(copies)

    def normed(group):
        at = group * GROUP
        normed_ref[group * rows : (group + 1) * rows, :] = normed_rows(
            states_ref[at : at + GROUP],
            live_at[...],
            at,
            transform_ref[...],
            bias_ref[...],
            gain_ref[...],
            shift_ref[...],
        )

    for copy in copies[:early]:
        copy.wait()

    @pl.when(always)
    def _():
        place_of(rows, live_at, tokens_ref)
        normed(0)

    for copy in copies[early:middle]:
        copy.wait()
    bring(decoder_hbm.at[:, pl.ds(chunk, next_ref.shape[1])], next_ref)

    @pl.when(always)
    def _():
        for group in range(groups):
            if group + 1 < groups:
                normed(group + 1)
            part = normed_ref[group * rows : (group + 1) * rows, :]
            pool(part, decoder_ref, decoder_bias_ref[:, :chunk], group, length, pooled)
        out_ref[:, :chunk] = keep_vocab(start_ref[0], pooled)
        depth = cand_ref.shape[0]
        wide = jnp.concatenate([cand_ref[...].astype(F32), jnp.zeros((depth, LANES - queries), F32)], axis=1)
        if depth < queries:
            wide = jnp.concatenate([wide, jnp.zeros((queries - depth, LANES), F32)], axis=0)
        out_ref[:, chunk:] = wide.astype(BF16)

    copies[-1].wait()


def chunk_kernel(begin, start_ref, normed_ref, decoder_ref, decoder_bias_ref, out_ref, pooled):
    queries, chunk = pooled.shape
    rows = normed_ref.shape[0] * GROUP // queries
    for group in range(queries // GROUP):
        part = normed_ref[group * rows : (group + 1) * rows, :]
        bias = decoder_bias_ref[:, begin : begin + chunk]
        pool(part, decoder_ref, bias, group, rows // GROUP, pooled)
    out_ref[...] = keep_vocab(start_ref[0] + begin, pooled)


def middle_kernel(
    begin, start_ref, normed_ref, decoder_ref, decoder_bias_ref, far_ref, out_ref, next_ref, pooled, sem
):
    last = begin + pooled.shape[1]
    copy = pltpu.make_async_copy(far_ref.at[:, pl.ds(last, next_ref.shape[1])], next_ref, sem)
    copy.start()

    @pl.when(start_ref[0] >= 0)
    def _():
        chunk_kernel(begin, start_ref, normed_ref, decoder_ref, decoder_bias_ref, out_ref, pooled)

    copy.wait()


def slot_queries(cand, base, tile_total):
    depth, queries = cand.shape
    row = lax.broadcasted_iota(jnp.int32, (tile_total, queries), 0) + base
    hits = jnp.zeros((tile_total, queries), F32)
    for place in range(depth):
        hits = jnp.where(cand[place : place + 1, :] == row, 1.0, hits)
    hits = hits.astype(BF16)
    mine = lax.broadcasted_iota(jnp.int32, (queries, queries), 0)
    other = lax.broadcasted_iota(jnp.int32, (queries, queries), 1)
    last = (((1,), (1,)), ((), ()))
    turned = lax.dot_general(
        jnp.where(mine == other, 1.0, 0.0).astype(BF16), hits, last, preferred_element_type=F32
    )
    before = lax.dot_general(
        jnp.where(other < mine, 1.0, 0.0).astype(BF16), hits, last, preferred_element_type=F32
    )
    rank = jnp.where(turned > 0.0, before, -1.0).astype(BF16)
    slots = tile_total * MOST
    tile = lax.broadcasted_iota(jnp.int32, (tile_total, slots), 0)
    spread = jnp.where(lax.broadcasted_iota(jnp.int32, (tile_total, slots), 1) // MOST == tile, 1.0, 0.0)
    wide = jnp.dot(rank, spread.astype(BF16), preferred_element_type=F32)
    want = (lax.broadcasted_iota(jnp.int32, (queries, slots), 1) % MOST).astype(F32)
    query = lax.broadcasted_iota(jnp.int32, (queries, slots), 0)
    return jnp.sum(jnp.where(wide == want, query, 0), axis=0, keepdims=True)


def docs_copies(far_ref, begin, target, sems):
    tile_total, blocks, _, _ = target.shape
    part = pl.ds(begin, blocks)
    return [
        pltpu.make_async_copy(far_ref.at[tile, part], target.at[tile], sems.at[tile]) for tile in range(tile_total)
    ]


def gather_weights(weight_refs, turned):
    queries = weight_refs[0].shape[0]
    for party, ref in enumerate(weight_refs):
        turned[party * queries : (party + 1) * queries, :] = ref[:, : turned.shape[1]]


def step_scores(step, begin, occupancy_ref, docs_ref, turned):
    tiles = LANES // MOST
    left = [
        jnp.concatenate(
            [
                jnp.where(occupancy_ref[tile, begin + block] != 0, docs_ref[tile, block], 0.0).astype(BF16)
                for block in range(docs_ref.shape[1])
            ],
            axis=1,
        )
        for tile in range(step * tiles, (step + 1) * tiles)
    ]
    return lax.dot_general(
        jnp.concatenate(left, axis=0), turned[...], (((1,), (1,)), ((), ())), preferred_element_type=F32
    )


def first_score_kernel(parties, depth, place_ref, occupancy_ref, far_ref, *refs):
    weight_refs = refs[:parties]
    after_ref, next_ref, slots_ref, turned, docs_ref, own_sems, next_sems = refs[parties:]
    tile_total, blocks, docs, _ = docs_ref.shape
    tiles = LANES // MOST
    rows = tiles * docs
    queries, chunk = weight_refs[0].shape[0], turned.shape[1]
    always = place_ref[0] >= 0
    own = docs_copies(far_ref, 0, docs_ref, own_sems)
    later = docs_copies(far_ref, blocks, next_ref, next_sems)
    queue = own + later

    def start(number):
        for copy in queue[:number]:
            copy.start()
        del queue[:number]

    start(3 * tiles)

    @pl.when(always)
    def _():
        gather_weights(weight_refs, turned)
        for party, ref in enumerate(weight_refs):
            cand = ref[:depth, chunk : chunk + queries].astype(F32).astype(jnp.int32)
            found = slot_queries(cand, place_ref[0] * tile_total, tile_total)
            slots_ref[party : party + 1, :] = found + party * queries % LANES

    start(2 * tiles)
    for step in range(tile_total // tiles):
        for copy in own[step * tiles : (step + 1) * tiles]:
            copy.wait()
        start(2 * tiles)

        @pl.when(always)
        def _(step=step):
            after_ref[step * rows : (step + 1) * rows, :] = step_scores(step, 0, occupancy_ref, docs_ref, turned)

    start(len(queue))
    for copy in later:
        copy.wait()


def middle_score_kernel(begin, parties, place_ref, occupancy_ref, docs_ref, before_ref, far_ref, *refs):
    weight_refs = refs[:parties]
    after_ref, next_ref, turned, sems = refs[parties:]
    tile_total, blocks, docs, _ = docs_ref.shape
    rows = LANES // MOST * docs
    copies = docs_copies(far_ref, begin + blocks, next_ref, sems)
    for copy in copies:
        copy.start()

    @pl.when(place_ref[0] >= 0)
    def _():
        gather_weights(weight_refs, turned)
        for step in range(tile_total * docs // rows):
            part = slice(step * rows, (step + 1) * rows)
            after_ref[part, :] = before_ref[part, :] + step_scores(step, begin, occupancy_ref, docs_ref, turned)

    for copy in copies:
        copy.wait()


def last_score_kernel(begin, parties, place_ref, occupancy_ref, docs_ref, before_ref, slots_ref, *refs):
    weight_refs = refs[:parties]
    out_ref, turned, total = refs[parties:]
    tile_total, _, docs, _ = docs_ref.shape
    tiles = LANES // MOST
    rows = tiles * docs
    queries = weight_refs[0].shape[0]
    term_count, share = total.shape[1], docs // total.shape[1]
    gather_weights(weight_refs, turned)
    lane = lax.broadcasted_iota(jnp.int32, (docs, LANES), 1) // MOST
    for step in range(tile_total // tiles):
        value = before_ref[step * rows : (step + 1) * rows, :]
        value = value + step_scores(step, begin, occupancy_ref, docs_ref, turned)
        for party in range(parties):
            column = party * queries // LANES * LANES
            source = slots_ref[party : party + 1, step * LANES : (step + 1) * LANES]
            source = jnp.broadcast_to(source, (docs, LANES))
            part = None
            for tile in range(tiles):
                held = value[tile * docs : (tile + 1) * docs, column : column + LANES]
                held = jnp.take_along_axis(held, source, axis=1, mode="promise_in_bounds")
                part = held if part is None else jnp.where(lane == tile, held, part)
            for term in range(term_count):
                total[party, term, step * share : (step + 1) * share, :] = part[term * share : (term + 1) * share]
    for party in range(parties):
        out_ref[place_ref[0] ^ party] = total[party].astype(BF16)


def ranks(cand, row, queries):
    depth, total = cand.shape
    hits = jnp.zeros((row.shape[0], total), F32)
    for place in range(depth):
        hits = jnp.where(cand[place : place + 1, :] == row, 1.0, hits)
    earlier = lax.broadcasted_iota(jnp.int32, (total, total), 0)
    later = lax.broadcasted_iota(jnp.int32, (total, total), 1)
    before = jnp.dot(
        hits.astype(BF16), jnp.where(earlier < later, 1.0, 0.0).astype(BF16), preferred_element_type=F32
    )
    return jnp.where(hits > 0.0, before, -1.0)


def choice_kernel(cand_ref, out_ref):
    queries = cand_ref.shape[1]
    groups = out_ref.shape[0]
    tiles = LANES // MOST
    cand = cand_ref[...]
    rank = ranks(cand, lax.broadcasted_iota(jnp.int32, (groups * tiles, queries), 0), queries)
    slot = lax.broadcasted_iota(jnp.int32, (LANES, tiles * queries), 0)
    for group in range(groups):
        want = [rank[group * tiles + k : group * tiles + k + 1] for k in range(tiles)]
        want = [jnp.where(w >= 0.0, w + k * MOST, -1.0) for k, w in enumerate(want)]
        want = jnp.concatenate(want, axis=1).astype(jnp.int32)
        out_ref[group] = jnp.where(slot == want, 1.0, 0.0).astype(BF16)


def final_kernel(cand_ref, choice_ref, got_ref, out_ref):
    docs_n, term_count, rows, _ = got_ref.shape
    depth, share, queries = out_ref.shape
    groups = rows // share
    tiles = LANES // MOST
    cand = cand_ref[...]
    twice = jnp.concatenate([cand, cand], axis=1)
    lane = lax.broadcasted_iota(jnp.int32, (1, 2 * queries), 1) // queries
    result = [jnp.zeros((share, 2 * queries), F32) for _ in range(depth)]
    for doc in range(docs_n):
        summed = got_ref[doc, 0].astype(F32)
        for term in range(1, term_count):
            summed = summed + got_ref[doc, term].astype(F32)
        for group in range(groups):
            first = (doc * groups + group) * tiles
            value = summed[group * share : (group + 1) * share]
            high = value.astype(BF16)
            low = (value - high.astype(F32)).astype(BF16)
            both = jnp.concatenate([high, low], axis=0)
            moved = jnp.dot(both, choice_ref[doc * groups + group], preferred_element_type=F32)
            moved = moved[:share] + moved[share:]
            for pair in range(tiles // 2):
                held = moved[:, pair * 2 * queries : (pair + 1) * 2 * queries]
                name = first + pair * 2 + lane
                for place in range(depth):
                    result[place] = jnp.where(twice[place : place + 1] == name, held, result[place])
    for place in range(depth):
        out_ref[place] = result[place][:, :queries] + result[place][:, queries:]


def body(
    query_states,
    token_ids,
    transform_weight,
    transform_bias,
    norm_gain,
    norm_bias,
    decoder_weight,
    decoder_bias,
    candidates,
    occupancy,
    doc_blocks,
):
    query_count, length, width = query_states.shape
    vocab = decoder_weight.shape[1]
    tile_local, blocks, docs, terms = doc_blocks.shape
    depth = candidates.shape[1]
    term_index, doc_index = lax.axis_index("term"), lax.axis_index("doc")
    doc_count, term_count = lax.axis_size("doc"), lax.axis_size("term")
    share = docs // term_count
    all_queries = doc_count * query_count
    tiles = LANES // MOST
    steps = tile_local // tiles
    cuts = (0, blocks // 3, blocks * 11 // 15, blocks)
    few = [cuts[k + 1] - cuts[k] for k in range(3)]
    chunks = [count * terms for count in few]
    begins = [cut * terms for cut in cuts[:3]]
    cand = candidates.T
    start = (term_index * vocab).reshape(1)
    place = doc_index.reshape(1)
    rows = query_count * length
    far, near = pltpu.HBM, pltpu.VMEM

    def put(space, *operands):
        return [pltpu.with_memory_space_constraint(operand, space) for operand in operands]

    def call(name, kernel, in_specs, out_shape, scratch, macs, limit, operands):
        return pl.pallas_call(
            kernel,
            in_specs=in_specs,
            out_specs=jax.tree.map(lambda _: WHOLE, out_shape),
            out_shape=out_shape,
            scratch_shapes=scratch,
            cost_estimate=pl.CostEstimate(flops=2 * macs, bytes_accessed=10**6, transcendentals=0),
            compiler_params=pltpu.CompilerParams(vmem_limit_bytes=limit),
            name=name,
        )(*operands)

    def next_docs(at):
        return near((tile_local, few[at], docs, terms), BF16)

    def pooled(at):
        return pltpu.VMEM((query_count, chunks[at]), F32)

    def turned(at):
        return pltpu.VMEM((all_queries, chunks[at]), BF16)

    def piece(at):
        return jax.ShapeDtypeStruct((query_count, chunks[at]), BF16)

    signals = pltpu.SemaphoreType.DMA((tile_local,))
    running = near((tile_local * docs, all_queries), F32)
    expand_macs = [rows * width * chunk for chunk in chunks]
    score_macs = [4 * tile_local * docs * chunk * all_queries for chunk in chunks]
    xor = [[(i, i ^ k) for i in range(doc_count)] for k in range(doc_count)]

    def spread(own, after):
        held = [own] + [None] * (doc_count - 1)
        bit, known = doc_count // 2, [0]
        while bit:
            for k in list(known):
                held[k | bit] = lax.ppermute(held[k], "doc", xor[bit])
                known.append(k | bit)
            if bit == doc_count // 2:
                held[bit], _ = lax.optimization_barrier((held[bit], after))
            bit //= 2
        return held

    first, normed, decoder, all_bias = call(
        "expand_first",
        first_kernel,
        [SCALARS] + [FAR] * 9,
        [
            jax.ShapeDtypeStruct((query_count, chunks[0] + LANES), BF16),
            near((rows, width), BF16),
            near((width, chunks[1]), BF16),
            near((1, vocab), F32),
        ],
        [
            pltpu.VMEM(query_states.shape, BF16),
            pltpu.VMEM(transform_weight.shape, BF16),
            pltpu.VMEM((width, chunks[0]), BF16),
            pltpu.VMEM((1, width), F32),
            pltpu.VMEM((1, width), F32),
            pltpu.VMEM((1, width), F32),
            pltpu.VMEM((length, query_count), jnp.int32),
            pltpu.VMEM(cand.shape, jnp.int32),
            pltpu.VMEM((GROUP * length, query_count), F32),
            pooled(0),
            pltpu.SemaphoreType.DMA((11,)),
        ],
        rows * width * width + expand_macs[0],
        13 << 20,
        [start]
        + put(
            far,
            query_states,
            token_ids.T,
            transform_weight,
            transform_bias,
            norm_gain,
            norm_bias,
            decoder_weight,
            decoder_bias,
            cand,
        ),
    )
    middle, decoder = call(
        "expand_middle",
        functools.partial(middle_kernel, begins[1]),
        [SCALARS] + [WHOLE] * 3 + [FAR],
        [piece(1), near((width, chunks[2]), BF16)],
        [pooled(1), pltpu.SemaphoreType.DMA(())],
        expand_macs[1],
        7 << 20,
        [start, *put(near, normed, decoder, all_bias), *put(far, decoder_weight)],
    )
    first_all = spread(first, middle)
    last = call(
        "expand_last",
        functools.partial(chunk_kernel, begins[2]),
        [SCALARS] + [WHOLE] * 3,
        piece(2),
        [pooled(2)],
        expand_macs[2],
        7 << 20,
        [start, *put(near, normed, decoder, all_bias)],
    )
    scores, near_docs, slots = call(
        "score_first",
        functools.partial(first_score_kernel, doc_count, depth),
        [SCALARS] * 2 + [FAR] + [WHOLE] * doc_count,
        [running, next_docs(1), near((doc_count, tile_local * MOST), jnp.int32)],
        [turned(0), pltpu.VMEM((tile_local, few[0], docs, terms), BF16), signals, signals],
        score_macs[0],
        14 << 20,
        [place, occupancy, *put(far, doc_blocks), *first_all],
    )
    last_all = spread(last, scores)
    middle_all = spread(middle, last)
    scores, near_docs = call(
        "score_middle",
        functools.partial(middle_score_kernel, cuts[1], doc_count),
        [SCALARS] * 2 + [WHOLE] * 2 + [FAR] + [WHOLE] * doc_count,
        [running, next_docs(2)],
        [turned(1), signals],
        score_macs[1],
        8 << 20,
        [place, occupancy, *put(near, near_docs, scores), *put(far, doc_blocks), *middle_all],
    )
    sent = call(
        "score_last",
        functools.partial(last_score_kernel, cuts[2], doc_count),
        [SCALARS] * 2 + [WHOLE] * (3 + doc_count),
        jax.ShapeDtypeStruct((doc_count, term_count, steps * share, LANES), BF16),
        [turned(2), pltpu.VMEM((doc_count, term_count, steps * share, LANES), F32)],
        score_macs[2],
        8 << 20,
        [place, occupancy, *put(near, near_docs, scores, slots), *last_all],
    )
    weights = jnp.concatenate([first[:, : chunks[0]], middle, last], axis=1)

    everyone = doc_count * term_count
    got = lax.all_to_all(
        sent.reshape(everyone, steps * share, LANES), ("doc", "term"), split_axis=0, concat_axis=0, tiled=True
    ).reshape(doc_count, term_count, steps * share, LANES)
    choices = call(
        "choices",
        choice_kernel,
        [WHOLE],
        jax.ShapeDtypeStruct((doc_count * steps, LANES, tiles * query_count), BF16),
        [],
        10**6,
        8 << 20,
        [cand],
    )
    scores = call(
        "place",
        final_kernel,
        [WHOLE] * 3,
        jax.ShapeDtypeStruct((depth, share, query_count), F32),
        [],
        10**6,
        8 << 20,
        [cand, choices, got],
    )
    return weights, scores.transpose(2, 0, 1)


def solution(mesh):
    placed = (
        P("doc", None, None),
        P("doc", None),
        P(),
        P(),
        P(),
        P(),
        P(None, "term"),
        P("term"),
        P("doc", None),
        P("doc", "term"),
        P("doc", "term", None, None),
    )
    return jax.shard_map(
        body,
        mesh=mesh,
        in_specs=placed,
        out_specs=(P("doc", "term"), P("doc", None, "term")),
        check_vma=False,
    )
```

time: 65.3 us -> 62.8 us (0.962)
  waiting for transfers between devices: 17.9 us -> 16.3 us
  Pallas kernels: 34.3 us -> 33.3 us
    ppermute x9, waiting for transfers between devices: 2.38 us -> 1.32 us  [spread(): held[k | bit] = lax.ppermute(held[k], 'doc', xor[bit])]
    pallas_call x7 -> x8, Pallas kernels: 34.3 us -> 33.3 us  [call(): pl.pallas_call(kernel, in_specs=in_specs, out_specs=jax.tree.map(lambda _...]
    ppermute x9, starting transfers between devices: 5.5 us -> 6.27 us  [spread(): held[k | bit] = lax.ppermute(held[k], 'doc', xor[bit])]
  transfers between devices with their start and end apart: 10 -> 10, of which waited for: 4 -> 2; matrix products, arithmetic and copies ran while one was open for 1% -> 1% of each run, Pallas kernels for 27% -> 28%
where the time goes in v3:
time: 62.8 us; the launch traced here: 62.4 us
  Pallas kernels  33.3 us (53%)
  waiting for transfers between devices  16.3 us (26%)
  starting transfers between devices  11.2 us (18%)
  other arithmetic  0.81 us (1%)
  between operations  0.76 us (1%)
    pallas_call x8, Pallas kernels, call(): pl.pallas_call(kernel, in_specs=in_specs, out_specs=jax.tree.map(lambda _...  33.3 us
    all_to_all x1, waiting for transfers between devices, body(): lax.all_to_all(sent.reshape(everyone, steps * share, LANES), ('doc', 'ter...  15 us
    ppermute x9, starting transfers between devices, spread(): held[k | bit] = lax.ppermute(held[k], 'doc', xor[bit])  6.27 us
    all_to_all x1, starting transfers between devices, body(): lax.all_to_all(sent.reshape(everyone, steps * share, LANES), ('doc', 'ter...  4.97 us
    ppermute x9, waiting for transfers between devices, spread(): held[k | bit] = lax.ppermute(held[k], 'doc', xor[bit])  1.32 us
  transfers between devices with their start and end apart: 10, of which 2 were waited for; matrix products, arithmetic and copies ran while one was open for 1% of the time, Pallas kernels for 28%

profile of v3, /device:TPU:0, one launch (start us, length us, event | category | flops | bytes accessed | tf_op | source)
XLA Modules:
  0.0 62.4 jit_solution(11826200434638298860)
XLA Ops:
  0.6 10.9 %expand_first.1 = (bf16[64,1408]{1,0:T(8,128)(2,1)S(1)}, bf16[2048,768]{1,0:T(8,128)(2,1)S(1)}, bf16[768,1536]{1,0:T(8,128)(2,1)S(1)}, f32[1,3840]{1,0:T(1,128)S(1)}) custom-call(s32[1]{0:T(128)} %bitcast.start_ref, bf16[64,32,768]{2,1,0:T(8,128)(2,1)} %states_hbm.1, s32[32,64]{1,0:T(8,128)} %bitcast.12, bf16[768,768]{1,0:T(8,128)(2,1)} %transform_hbm.1, ...), custom_call_target="tpu_custom_call" | custom-call | flops 6442450944 | bytes 1000000 | tf_op jit(solution)/shard_map/expand_first/pallas_call | solution.py:427
  11.5 3.0 %collective-permute-start.1 = (bf16[64,1408]{1,0:T(8,128)(2,1)S(1)}, bf16[64,1408]{1,0:T(8,128)(2,1)S(1)}, u32[]{:S(2)}, u32[]{:S(2)}) collective-permute-start(bf16[64,1408]{1,0:T(8,128)(2,1)S(1)} %get-tuple-element.16.refs_0_), channel_id=1, source_target_pairs={{0,16},{8,24},{16,0},{24,8},{1,17},{9,25},{17,1},{25,9},{2,18},{10... | collective-permute-start | bytes 540680 | tf_op jit(solution)/shard_map/ppermute | solution.py:461
  14.5 0.0 collective-permute-start
  14.5 5.1 %expand_middle.1 = (bf16[64,1536]{1,0:T(8,128)(2,1)S(1)}, bf16[768,1024]{1,0:T(8,128)(2,1)S(1)}) custom-call(s32[1]{0:T(128)} %bitcast.start_ref, bf16[2048,768]{1,0:T(8,128)(2,1)S(1)} %get-tuple-element.17.normed_ref, bf16[768,1536]{1,0:T(8,128)(2,1)S(1)} %get-tuple-element.18.decoder_ref, f32[1,3840]{1,0:T(1,128)S(1)} %get-tuple-element.19.decoder_bias_ref, ...), custom_call_target="tpu_custom_call" | custom-call | flops 4831838208 | bytes 1000000 | tf_op jit(solution)/shard_map/expand_middle/pallas_call | solution.py:427
  19.6 0.3 collective-permute-start.4
  19.9 0.3 collective-permute-start.3
  20.2 0.0 collective-permute-done.1.refs_2_
  20.2 0.2 collective-permute-start.2
  20.5 3.4 %expand_last.1.refs_0_ = bf16[64,1024]{1,0:T(8,128)(2,1)S(1)} custom-call(s32[1]{0:T(128)} %bitcast.start_ref, bf16[2048,768]{1,0:T(8,128)(2,1)S(1)} %get-tuple-element.17.normed_ref, bf16[768,1024]{1,0:T(8,128)(2,1)S(1)} %get-tuple-element.21.decoder_ref, f32[1,3840]{1,0:T(1,128)S(1)} %get-tuple-element.19.decoder_bias_ref), custom_call_target="tpu_custom_call" | custom-call | flops 3221225472 | bytes 1000000 | tf_op jit(solution)/shard_map/expand_last/pallas_call | solution.py:427
  23.9 1.8 %collective-permute-start.7 = (bf16[64,1024]{1,0:T(8,128)(2,1)S(1)}, bf16[64,1024]{1,0:T(8,128)(2,1)S(1)}, u32[]{:S(2)}, u32[]{:S(2)}) collective-permute-start(bf16[64,1024]{1,0:T(8,128)(2,1)S(1)} %expand_last.1.refs_0_), channel_id=1, source_target_pairs={{0,16},{8,24},{16,0},{24,8},{1,17},{9,25},{17,1},{25,9},{2,18},{10... | collective-permute-start | bytes 393224 | tf_op jit(solution)/shard_map/ppermute | solution.py:461
  25.7 1.3 %collective-permute-done.4.refs_2_ = bf16[64,1536]{1,0:T(8,128)(2,1)S(1)} collective-permute-done((bf16[64,1536]{1,0:T(8,128)(2,1)S(1)}, bf16[64,1536]{1,0:T(8,128)(2,1)S(1)}, u32[]{:S(2)}, u32[]{:S(2)}) %collective-permute-start.4) | collective-permute-done | bytes 196640 | tf_op jit(solution)/shard_map/ppermute | solution.py:461
  27.0 0.0 collective-permute-start.6
  27.0 0.0 collective-permute-done.refs_1_
  27.0 0.5 collective-permute-start.5
  27.5 0.0 collective-permute-done.2.refs_3_
  27.5 0.0 copy-done.1
  27.5 5.4 %score_first.1 = (f32[2048,256]{1,0:T(8,128)S(1)}, bf16[16,12,128,128]{3,2,1,0:T(8,128)(2,1)S(1)}, s32[4,512]{1,0:T(4,128)S(1)}) custom-call(s32[1]{0:T(128)} %bitcast.3.place_ref, s32[16,30]{1,0:T(8,128)S(1)} %copy-done.1, bf16[16,30,128,128]{3,2,1,0:T(8,128)(2,1)} %far_ref.5, bf16[64,1408]{1,0:T(8,128)(2,1)S(1)} %get-tuple-element.16.refs_0_, ...), custom_call_target="tpu_custom_call" | custom-call | flops 5368709120 | bytes 1000000 | tf_op jit(solution)/shard_map/score_first/pallas_call | solution.py:427
  32.9 0.0 collective-permute-done.7.refs_2_
  32.9 0.1 collective-permute-start.8
  33.0 0.0 collective-permute-done.3.refs_1_
  33.0 0.0 collective-permute-done.5.refs_3_
  33.0 2.9 %score_middle.1 = (f32[2048,256]{1,0:T(8,128)S(1)}, bf16[16,8,128,128]{3,2,1,0:T(8,128)(2,1)S(1)}) custom-call(s32[1]{0:T(128)} %bitcast.3.place_ref, s32[16,30]{1,0:T(8,128)S(1)} %copy-done.1, bf16[16,12,128,128]{3,2,1,0:T(8,128)(2,1)S(1)} %get-tuple-element.23.docs_ref, f32[2048,256]{1,0:T(8,128)S(1)} %get-tuple-element.24.before_ref, ...), custom_call_target="tpu_custom_call" | custom-call | flops 6442450944 | bytes 1000000 | tf_op jit(solution)/shard_map/score_middle/pallas_call | solution.py:427
  36.0 0.0 collective-permute-done.6.refs_1_
  36.0 0.0 collective-permute-done.8.refs_3_
  36.0 0.0 copy-start
  36.0 3.3 %score_last.1 = bf16[4,8,64,128]{3,2,1,0:T(8,128)(2,1)} custom-call(s32[1]{0:T(128)} %bitcast.3.place_ref, s32[16,30]{1,0:T(8,128)S(1)} %copy-done.1, bf16[16,8,128,128]{3,2,1,0:T(8,128)(2,1)S(1)} %get-tuple-element.26.docs_ref, f32[2048,256]{1,0:T(8,128)S(1)} %get-tuple-element.27.before_ref, s32[4,512]{1,0:T(4,128)S(1)} %get-tuple-element.28.slots_ref, ...), custom_call_target="tpu_custom_call" | custom-call | flops 4294967296 | bytes 1000000 | tf_op jit(solution)/shard_map/score_last/pallas_call | solution.py:427
  39.3 5.0 %all-to-all-start = ((bf16[32,64,128]{2,1,0:T(8,128)(2,1)}), bf16[32,64,128]{2,1,0:T(8,128)(2,1)S(1)}, u32[]{:S(2)}, u32[]{:S(2)}) async-start(bf16[32,64,128]{2,1,0:T(8,128)(2,1)} %bitcast.4), calls=%async_computation | async-start | bytes 1048576 | tf_op jit(solution)/shard_map/all_to_all | solution.py:563
  44.3 0.0 copy-done
  44.4 0.5 choices.1.choice_ref
  44.9 0.8 %pad_maximum_fusion = bf16[64,3840]{1,0:T(8,128)(2,1)} fusion(bf16[64,1024]{1,0:T(8,128)(2,1)S(1)} %expand_last.1.refs_0_, bf16[64,1536]{1,0:T(8,128)(2,1)S(1)} %get-tuple-element.20.refs_0_, bf16[64,1280]{1,0:T(8,128)(2,1)S(1)} %slice.3), kind=kLoop, calls=%fused_computation | loop fusion | flops 1474560 | bytes 983040 | tf_op jit(solution)/shard_map/concatenate | solution.py:560
  45.7 15.0 %all-to-all-done = bf16[32,64,128]{2,1,0:T(8,128)(2,1)S(1)} async-done(((bf16[32,64,128]{2,1,0:T(8,128)(2,1)}), bf16[32,64,128]{2,1,0:T(8,128)(2,1)S(1)}, u32[]{:S(2)}, u32[]{:S(2)}) %all-to-all-start) | async-done | bytes 524320 | tf_op jit(solution)/shard_map/all_to_all | solution.py:563
  60.7 1.8 %place.1 = f32[32,16,64]{2,1,0:T(8,128)} custom-call(s32[32,64]{1,0:T(8,128)S(1)} %bitcast.10, bf16[16,128,256]{2,1,0:T(8,128)(2,1)S(1)} %choices.1.choice_ref, bf16[4,8,64,128]{3,2,1,0:T(8,128)(2,1)S(1)} %bitcast.7), custom_call_target="tpu_custom_call" | custom-call | flops 2000000 | bytes 1000000 | tf_op jit(solution)/shard_map/place/pallas_call | solution.py:427
  (2 shorter events, 0.0 us)
Async XLA Ops:
  11.5 8.8 %collective-permute-start.1 = (bf16[64,1408]{1,0:T(8,128)(2,1)S(1)}, bf16[64,1408]{1,0:T(8,128)(2,1)S(1)}, u32[]{:S(2)}, u32[]{:S(2)}) collective-permute-start(bf16[64,1408]{1,0:T(8,128)(2,1)S(1)} %get-tuple-element.16.refs_0_), channel_id=1, source_target_pairs={{0,16},{8,24},{16,0},{24,8},{1,17},{9,25},{17,1},{25,9},{2,18},{10... | collective-permute-start | bytes 540680 | tf_op jit(solution)/shard_map/ppermute | solution.py:461
  14.5 12.5 %collective-permute-start = (bf16[64,1408]{1,0:T(8,128)(2,1)S(1)}, bf16[64,1408]{1,0:T(8,128)(2,1)S(1)}, u32[]{:S(2)}, u32[]{:S(2)}) collective-permute-start(bf16[64,1408]{1,0:T(8,128)(2,1)S(1)} %get-tuple-element.16.refs_0_), channel_id=1, source_target_pairs={{0,8},{8,0},{16,24},{24,16},{1,9},{9,1},{17,25},{25,17},{2,10},{10... | collective-permute-start | bytes 540680 | tf_op jit(solution)/shard_map/ppermute | solution.py:461
  19.6 7.4 %collective-permute-start.4 = (bf16[64,1536]{1,0:T(8,128)(2,1)S(1)}, bf16[64,1536]{1,0:T(8,128)(2,1)S(1)}, u32[]{:S(2)}, u32[]{:S(2)}) collective-permute-start(bf16[64,1536]{1,0:T(8,128)(2,1)S(1)} %get-tuple-element.20.refs_0_), channel_id=1, source_target_pairs={{0,16},{8,24},{16,0},{24,8},{1,17},{9,25},{17,1},{25,9},{2,18},{10... | collective-permute-start | bytes 589832 | tf_op jit(solution)/shard_map/ppermute | solution.py:461
  19.9 13.1 %collective-permute-start.3 = (bf16[64,1536]{1,0:T(8,128)(2,1)S(1)}, bf16[64,1536]{1,0:T(8,128)(2,1)S(1)}, u32[]{:S(2)}, u32[]{:S(2)}) collective-permute-start(bf16[64,1536]{1,0:T(8,128)(2,1)S(1)} %get-tuple-element.20.refs_0_), channel_id=1, source_target_pairs={{0,8},{8,0},{16,24},{24,16},{1,9},{9,1},{17,25},{25,17},{2,10},{10... | collective-permute-start | bytes 589832 | tf_op jit(solution)/shard_map/ppermute | solution.py:461
  20.2 7.3 %collective-permute-start.2 = (bf16[64,1408]{1,0:T(8,128)(2,1)S(1)}, bf16[64,1408]{1,0:T(8,128)(2,1)S(1)}, u32[]{:S(2)}, u32[]{:S(2)}) collective-permute-start(bf16[64,1408]{1,0:T(8,128)(2,1)S(1)} %collective-permute-done.1.refs_2_), channel_id=1, source_target_pairs={{0,8},{8,0},{16,24},{24,16},{1,9},{9,1},{17,25},{25,17},{2,10},{10... | collective-permute-start | bytes 540680 | tf_op jit(solution)/shard_map/ppermute | solution.py:461
  20.4 7.1 %copy-start.1 = (s32[16,30]{1,0:T(8,128)S(1)}, s32[16,30]{1,0:T(8,128)}, u32[]{:S(2)}) copy-start(s32[16,30]{1,0:T(8,128)} %occupancy_ref.5) | copy-start | bytes 5764
  23.9 9.0 %collective-permute-start.7 = (bf16[64,1024]{1,0:T(8,128)(2,1)S(1)}, bf16[64,1024]{1,0:T(8,128)(2,1)S(1)}, u32[]{:S(2)}, u32[]{:S(2)}) collective-permute-start(bf16[64,1024]{1,0:T(8,128)(2,1)S(1)} %expand_last.1.refs_0_), channel_id=1, source_target_pairs={{0,16},{8,24},{16,0},{24,8},{1,17},{9,25},{17,1},{25,9},{2,18},{10... | collective-permute-start | bytes 393224 | tf_op jit(solution)/shard_map/ppermute | solution.py:461
  27.0 9.0 %collective-permute-start.6 = (bf16[64,1024]{1,0:T(8,128)(2,1)S(1)}, bf16[64,1024]{1,0:T(8,128)(2,1)S(1)}, u32[]{:S(2)}, u32[]{:S(2)}) collective-permute-start(bf16[64,1024]{1,0:T(8,128)(2,1)S(1)} %expand_last.1.refs_0_), channel_id=1, source_target_pairs={{0,8},{8,0},{16,24},{24,16},{1,9},{9,1},{17,25},{25,17},{2,10},{10... | collective-permute-start | bytes 393224 | tf_op jit(solution)/shard_map/ppermute | solution.py:461
  27.0 6.0 %collective-permute-start.5 = (bf16[64,1536]{1,0:T(8,128)(2,1)S(1)}, bf16[64,1536]{1,0:T(8,128)(2,1)S(1)}, u32[]{:S(2)}, u32[]{:S(2)}) collective-permute-start(bf16[64,1536]{1,0:T(8,128)(2,1)S(1)} %collective-permute-done.4.refs_2_), channel_id=1, source_target_pairs={{0,8},{8,0},{16,24},{24,16},{1,9},{9,1},{17,25},{25,17},{2,10},{10... | collective-permute-start | bytes 589832 | tf_op jit(solution)/shard_map/ppermute | solution.py:461
  32.9 3.1 %collective-permute-start.8 = (bf16[64,1024]{1,0:T(8,128)(2,1)S(1)}, bf16[64,1024]{1,0:T(8,128)(2,1)S(1)}, u32[]{:S(2)}, u32[]{:S(2)}) collective-permute-start(bf16[64,1024]{1,0:T(8,128)(2,1)S(1)} %collective-permute-done.7.refs_2_), channel_id=1, source_target_pairs={{0,8},{8,0},{16,24},{24,16},{1,9},{9,1},{17,25},{25,17},{2,10},{10... | collective-permute-start | bytes 393224 | tf_op jit(solution)/shard_map/ppermute | solution.py:461
  36.0 8.3 %copy-start = (s32[64,32]{0,1:T(8,128)S(1)}, s32[64,32]{0,1:T(8,128)}, u32[]{:S(2)}) copy-start(s32[64,32]{0,1:T(8,128)} %param.19) | copy-start | bytes 24580
  39.3 21.3 %all-to-all-start = ((bf16[32,64,128]{2,1,0:T(8,128)(2,1)}), bf16[32,64,128]{2,1,0:T(8,128)(2,1)S(1)}, u32[]{:S(2)}, u32[]{:S(2)}) async-start(bf16[32,64,128]{2,1,0:T(8,128)(2,1)} %bitcast.4), calls=%async_computation | async-start | bytes 1048576 | tf_op jit(solution)/shard_map/all_to_all | solution.py:563

commit v4 on v3

--- a/solution.py
+++ b/solution.py
@@ -169,20 +169,6 @@
     out_ref[...] = keep_vocab(start_ref[0] + begin, pooled)
 
 
-def middle_kernel(
-    begin, start_ref, normed_ref, decoder_ref, decoder_bias_ref, far_ref, out_ref, next_ref, pooled, sem
-):
-    last = begin + pooled.shape[1]
-    copy = pltpu.make_async_copy(far_ref.at[:, pl.ds(last, next_ref.shape[1])], next_ref, sem)
-    copy.start()
-
-    @pl.when(start_ref[0] >= 0)
-    def _():
-        chunk_kernel(begin, start_ref, normed_ref, decoder_ref, decoder_bias_ref, out_ref, pooled)
-
-    copy.wait()
-
-
 def slot_queries(cand, base, tile_total):
     depth, queries = cand.shape
     row = lax.broadcasted_iota(jnp.int32, (tile_total, queries), 0) + base
@@ -279,26 +265,6 @@
 
     start(len(queue))
     for copy in later:
-        copy.wait()
-
-
-def middle_score_kernel(begin, parties, place_ref, occupancy_ref, docs_ref, before_ref, far_ref, *refs):
-    weight_refs = refs[:parties]
-    after_ref, next_ref, turned, sems = refs[parties:]
-    tile_total, blocks, docs, _ = docs_ref.shape
-    rows = LANES // MOST * docs
-    copies = docs_copies(far_ref, begin + blocks, next_ref, sems)
-    for copy in copies:
-        copy.start()
-
-    @pl.when(place_ref[0] >= 0)
-    def _():
-        gather_weights(weight_refs, turned)
-        for step in range(tile_total * docs // rows):
-            part = slice(step * rows, (step + 1) * rows)
-            after_ref[part, :] = before_ref[part, :] + step_scores(step, begin, occupancy_ref, docs_ref, turned)
-
-    for copy in copies:
         copy.wait()
 
 
@@ -327,7 +293,7 @@
             for term in range(term_count):
                 total[party, term, step * share : (step + 1) * share, :] = part[term * share : (term + 1) * share]
     for party in range(parties):
-        out_ref[place_ref[0] ^ party] = total[party].astype(BF16)
+        out_ref[:, place_ref[0] ^ party] = total[party].astype(BF16)
 
 
 def ranks(cand, row, queries):
@@ -358,7 +324,7 @@
 
 
 def final_kernel(cand_ref, choice_ref, got_ref, out_ref):
-    docs_n, term_count, rows, _ = got_ref.shape
+    term_count, docs_n, rows, _ = got_ref.shape
     depth, share, queries = out_ref.shape
     groups = rows // share
     tiles = LANES // MOST
@@ -367,9 +333,9 @@
     lane = lax.broadcasted_iota(jnp.int32, (1, 2 * queries), 1) // queries
     result = [jnp.zeros((share, 2 * queries), F32) for _ in range(depth)]
     for doc in range(docs_n):
-        summed = got_ref[doc, 0].astype(F32)
+        summed = got_ref[0, doc].astype(F32)
         for term in range(1, term_count):
-            summed = summed + got_ref[doc, term].astype(F32)
+            summed = summed + got_ref[term, doc].astype(F32)
         for group in range(groups):
             first = (doc * groups + group) * tiles
             value = summed[group * share : (group + 1) * share]
@@ -410,10 +376,10 @@
     all_queries = doc_count * query_count
     tiles = LANES // MOST
     steps = tile_local // tiles
-    cuts = (0, blocks // 3, blocks * 11 // 15, blocks)
-    few = [cuts[k + 1] - cuts[k] for k in range(3)]
+    cuts = (0, blocks // 2, blocks)
+    few = [cuts[k + 1] - cuts[k] for k in range(2)]
     chunks = [count * terms for count in few]
-    begins = [cut * terms for cut in cuts[:3]]
+    begins = [cut * terms for cut in cuts[:2]]
     cand = candidates.T
     start = (term_index * vocab).reshape(1)
     place = doc_index.reshape(1)
@@ -489,7 +455,7 @@
             pltpu.SemaphoreType.DMA((11,)),
         ],
         rows * width * width + expand_macs[0],
-        13 << 20,
+        16 << 20,
         [start]
         + put(
             far,
@@ -504,27 +470,17 @@
             cand,
         ),
     )
-    middle, decoder = call(
-        "expand_middle",
-        functools.partial(middle_kernel, begins[1]),
-        [SCALARS] + [WHOLE] * 3 + [FAR],
-        [piece(1), near((width, chunks[2]), BF16)],
-        [pooled(1), pltpu.SemaphoreType.DMA(())],
+    last = call(
+        "expand_last",
+        functools.partial(chunk_kernel, begins[1]),
+        [SCALARS] + [WHOLE] * 3,
+        piece(1),
+        [pooled(1)],
         expand_macs[1],
         7 << 20,
-        [start, *put(near, normed, decoder, all_bias), *put(far, decoder_weight)],
-    )
-    first_all = spread(first, middle)
-    last = call(
-        "expand_last",
-        functools.partial(chunk_kernel, begins[2]),
-        [SCALARS] + [WHOLE] * 3,
-        piece(2),
-        [pooled(2)],
-        expand_macs[2],
-        7 << 20,
         [start, *put(near, normed, decoder, all_bias)],
     )
+    first_all = spread(first, last)
     scores, near_docs, slots = call(
         "score_first",
         functools.partial(first_score_kernel, doc_count, depth),
@@ -532,37 +488,26 @@
         [running, next_docs(1), near((doc_count, tile_local * MOST), jnp.int32)],
         [turned(0), pltpu.VMEM((tile_local, few[0], docs, terms), BF16), signals, signals],
         score_macs[0],
-        14 << 20,
+        20 << 20,
         [place, occupancy, *put(far, doc_blocks), *first_all],
     )
     last_all = spread(last, scores)
-    middle_all = spread(middle, last)
-    scores, near_docs = call(
-        "score_middle",
-        functools.partial(middle_score_kernel, cuts[1], doc_count),
-        [SCALARS] * 2 + [WHOLE] * 2 + [FAR] + [WHOLE] * doc_count,
-        [running, next_docs(2)],
-        [turned(1), signals],
+    sent = call(
+        "score_last",
+        functools.partial(last_score_kernel, cuts[1], doc_count),
+        [SCALARS] * 2 + [WHOLE] * (3 + doc_count),
+        jax.ShapeDtypeStruct((term_count, doc_count, steps * share, LANES), BF16),
+        [turned(1), pltpu.VMEM((doc_count, term_count, steps * share, LANES), F32)],
         score_macs[1],
         8 << 20,
-        [place, occupancy, *put(near, near_docs, scores), *put(far, doc_blocks), *middle_all],
-    )
-    sent = call(
-        "score_last",
-        functools.partial(last_score_kernel, cuts[2], doc_count),
-        [SCALARS] * 2 + [WHOLE] * (3 + doc_count),
-        jax.ShapeDtypeStruct((doc_count, term_count, steps * share, LANES), BF16),
-        [turned(2), pltpu.VMEM((doc_count, term_count, steps * share, LANES), F32)],
-        score_macs[2],
-        8 << 20,
         [place, occupancy, *put(near, near_docs, scores, slots), *last_all],
     )
-    weights = jnp.concatenate([first[:, : chunks[0]], middle, last], axis=1)
+    weights = jnp.concatenate([first[:, : chunks[0]], last], axis=1)
 
     everyone = doc_count * term_count
     got = lax.all_to_all(
-        sent.reshape(everyone, steps * share, LANES), ("doc", "term"), split_axis=0, concat_axis=0, tiled=True
-    ).reshape(doc_count, term_count, steps * share, LANES)
+        sent.reshape(everyone, steps * share, LANES), ("term", "doc"), split_axis=0, concat_axis=0, tiled=True
+    ).reshape(term_count, doc_count, steps * share, LANES)
     choices = call(
         "choices",
         choice_kernel,

time: 62.8 us -> 61.8 us (0.984)
  starting transfers between devices: 11.2 us -> 10.3 us
    ppermute x9 -> x6, starting transfers between devices: 6.27 us -> 4.8 us  [spread(): held[k | bit] = lax.ppermute(held[k], 'doc', xor[bit])]
    all_to_all x1, waiting for transfers between devices: 15 us -> 14.2 us  [body(): lax.all_to_all(sent.reshape(everyone, steps * share, LANES), ('term', 'do...]
    pallas_call x8 -> x6, Pallas kernels: 33.3 us -> 33.7 us  [call(): pl.pallas_call(kernel, in_specs=in_specs, out_specs=jax.tree.map(lambda _...]
    ppermute x9 -> x6, waiting for transfers between devices: 1.32 us -> 1.65 us  [spread(): held[k | bit] = lax.ppermute(held[k], 'doc', xor[bit])]
  transfers between devices with their start and end apart: 10 -> 7, of which waited for: 2 -> 4; matrix products, arithmetic and copies ran while one was open for 1% -> 1% of each run, Pallas kernels for 28% -> 22%
where the time goes in v4:
time: 61.8 us; the launch traced here: 61.4 us
  Pallas kernels  33.7 us (55%)
  waiting for transfers between devices  15.8 us (26%)
  starting transfers between devices  10.3 us (17%)
  other arithmetic  0.81 us (1%)
  between operations  0.71 us (1%)
    pallas_call x6, Pallas kernels, call(): pl.pallas_call(kernel, in_specs=in_specs, out_specs=jax.tree.map(lambda _...  33.7 us
    all_to_all x1, waiting for transfers between devices, body(): lax.all_to_all(sent.reshape(everyone, steps * share, LANES), ('term', 'do...  14.2 us
    all_to_all x1, starting transfers between devices, body(): lax.all_to_all(sent.reshape(everyone, steps * share, LANES), ('term', 'do...  5.53 us
    ppermute x6, starting transfers between devices, spread(): held[k | bit] = lax.ppermute(held[k], 'doc', xor[bit])  4.8 us
    ppermute x6, waiting for transfers between devices, spread(): held[k | bit] = lax.ppermute(held[k], 'doc', xor[bit])  1.65 us
  transfers between devices with their start and end apart: 7, of which 4 were waited for; matrix products, arithmetic and copies ran while one was open for 1% of the time, Pallas kernels for 22%

profile of v4, /device:TPU:0, one launch (start us, length us, event | category | flops | bytes accessed | tf_op | source)
XLA Modules:
  0.0 61.4 jit_solution(9937729565014854529)
XLA Ops:
  0.6 13.7 %expand_first.1 = (bf16[64,2048]{1,0:T(8,128)(2,1)S(1)}, bf16[2048,768]{1,0:T(8,128)(2,1)S(1)}, bf16[768,1920]{1,0:T(8,128)(2,1)S(1)}, f32[1,3840]{1,0:T(1,128)S(1)}) custom-call(s32[1]{0:T(128)} %bitcast.start_ref, bf16[64,32,768]{2,1,0:T(8,128)(2,1)} %states_hbm.1, s32[32,64]{1,0:T(8,128)} %bitcast.12, bf16[768,768]{1,0:T(8,128)(2,1)} %transform_hbm.1, ...), custom_call_target="tpu_custom_call" | custom-call | flops 8455716864 | bytes 1000000 | tf_op jit(solution)/shard_map/expand_first/pallas_call | solution.py:393
  14.3 3.0 %collective-permute-start.1 = (bf16[64,2048]{1,0:T(8,128)(2,1)S(1)}, bf16[64,2048]{1,0:T(8,128)(2,1)S(1)}, u32[]{:S(2)}, u32[]{:S(2)}) collective-permute-start(bf16[64,2048]{1,0:T(8,128)(2,1)S(1)} %get-tuple-element.11.refs_0_), channel_id=1, source_target_pairs={{0,16},{8,24},{16,0},{24,8},{1,17},{9,25},{17,1},{25,9},{2,18},{10... | collective-permute-start | bytes 786440 | tf_op jit(solution)/shard_map/ppermute | solution.py:427
  17.3 0.0 collective-permute-start
  17.3 0.0 copy-start.1
  17.4 6.7 %expand_last.1.refs_0_ = bf16[64,1920]{1,0:T(8,128)(2,1)S(1)} custom-call(s32[1]{0:T(128)} %bitcast.start_ref, bf16[2048,768]{1,0:T(8,128)(2,1)S(1)} %get-tuple-element.12.normed_ref, bf16[768,1920]{1,0:T(8,128)(2,1)S(1)} %get-tuple-element.13.decoder_ref, f32[1,3840]{1,0:T(1,128)S(1)} %get-tuple-element.14.decoder_bias_ref), custom_call_target="tpu_custom_call" | custom-call | flops 6039797760 | bytes 1000000 | tf_op jit(solution)/shard_map/expand_last/pallas_call | solution.py:393
  24.1 0.0 collective-permute-done.1.refs_2_
  24.1 0.6 collective-permute-start.2
  24.6 0.7 %collective-permute-start.4 = (bf16[64,1920]{1,0:T(8,128)(2,1)S(1)}, bf16[64,1920]{1,0:T(8,128)(2,1)S(1)}, u32[]{:S(2)}, u32[]{:S(2)}) collective-permute-start(bf16[64,1920]{1,0:T(8,128)(2,1)S(1)} %expand_last.1.refs_0_), channel_id=1, source_target_pairs={{0,16},{8,24},{16,0},{24,8},{1,17},{9,25},{17,1},{25,9},{2,18},{10... | collective-permute-start | bytes 737288 | tf_op jit(solution)/shard_map/ppermute | solution.py:427
  25.4 0.2 collective-permute-start.3
  25.6 0.0 collective-permute-done.refs_1_
  25.6 0.2 collective-permute-done.2.refs_3_
  25.8 0.0 copy-done.1
  25.8 6.6 %score_first.1 = (f32[2048,256]{1,0:T(8,128)S(1)}, bf16[16,15,128,128]{3,2,1,0:T(8,128)(2,1)S(1)}, s32[4,512]{1,0:T(4,128)S(1)}) custom-call(s32[1]{0:T(128)} %bitcast.3.place_ref, s32[16,30]{1,0:T(8,128)S(1)} %copy-done.1, bf16[16,30,128,128]{3,2,1,0:T(8,128)(2,1)} %far_ref.1, bf16[64,2048]{1,0:T(8,128)(2,1)S(1)} %get-tuple-element.11.refs_0_, ...), custom_call_target="tpu_custom_call" | custom-call | flops 8053063680 | bytes 1000000 | tf_op jit(solution)/shard_map/score_first/pallas_call | solution.py:393
  32.4 0.2 collective-permute-done.4.refs_2_
  32.6 0.2 collective-permute-start.5
  32.8 0.0 collective-permute-done.3.refs_1_
  32.8 1.3 %collective-permute-done.5.refs_3_ = bf16[64,1920]{1,0:T(8,128)(2,1)S(1)} collective-permute-done((bf16[64,1920]{1,0:T(8,128)(2,1)S(1)}, bf16[64,1920]{1,0:T(8,128)(2,1)S(1)}, u32[]{:S(2)}, u32[]{:S(2)}) %collective-permute-start.5) | collective-permute-done | bytes 245792 | tf_op jit(solution)/shard_map/ppermute | solution.py:427
  34.1 0.0 copy-start
  34.1 4.5 %score_last.1 = bf16[8,4,64,128]{3,2,1,0:T(8,128)(2,1)} custom-call(s32[1]{0:T(128)} %bitcast.3.place_ref, s32[16,30]{1,0:T(8,128)S(1)} %copy-done.1, bf16[16,15,128,128]{3,2,1,0:T(8,128)(2,1)S(1)} %get-tuple-element.16.docs_ref, f32[2048,256]{1,0:T(8,128)S(1)} %get-tuple-element.17.before_ref, s32[4,512]{1,0:T(4,128)S(1)} %get-tuple-element.18.slots_ref, ...), custom_call_target="tpu_custom_call" | custom-call | flops 8053063680 | bytes 1000000 | tf_op jit(solution)/shard_map/score_last/pallas_call | solution.py:393
  38.6 5.5 %all-to-all-start = ((bf16[32,64,128]{2,1,0:T(8,128)(2,1)}), bf16[32,64,128]{2,1,0:T(8,128)(2,1)S(1)}, u32[]{:S(2)}, u32[]{:S(2)}) async-start(bf16[32,64,128]{2,1,0:T(8,128)(2,1)} %bitcast.4), calls=%async_computation | async-start | bytes 1048576 | tf_op jit(solution)/shard_map/all_to_all | solution.py:508
  44.1 0.0 copy-done
  44.1 0.5 choices.1.choice_ref
  44.6 0.8 %pad_maximum_fusion = bf16[64,3840]{1,0:T(8,128)(2,1)} fusion(bf16[64,1920]{1,0:T(8,128)(2,1)S(1)} %expand_last.1.refs_0_, bf16[64,1920]{1,0:T(8,128)(2,1)S(1)} %slice.3), kind=kLoop, calls=%fused_computation | loop fusion | flops 983040 | bytes 983040 | tf_op jit(solution)/shard_map/concatenate | solution.py:505
  45.4 14.2 %all-to-all-done = bf16[32,64,128]{2,1,0:T(8,128)(2,1)S(1)} async-done(((bf16[32,64,128]{2,1,0:T(8,128)(2,1)}), bf16[32,64,128]{2,1,0:T(8,128)(2,1)S(1)}, u32[]{:S(2)}, u32[]{:S(2)}) %all-to-all-start) | async-done | bytes 524320 | tf_op jit(solution)/shard_map/all_to_all | solution.py:508
  59.6 1.8 %place.1 = f32[32,16,64]{2,1,0:T(8,128)} custom-call(s32[32,64]{1,0:T(8,128)S(1)} %bitcast.10, bf16[16,128,256]{2,1,0:T(8,128)(2,1)S(1)} %choices.1.choice_ref, bf16[8,4,64,128]{3,2,1,0:T(8,128)(2,1)S(1)} %bitcast.7), custom_call_target="tpu_custom_call" | custom-call | flops 2000000 | bytes 1000000 | tf_op jit(solution)/shard_map/place/pallas_call | solution.py:393
  (1 shorter events, 0.0 us)
Async XLA Ops:
  14.3 9.7 %collective-permute-start.1 = (bf16[64,2048]{1,0:T(8,128)(2,1)S(1)}, bf16[64,2048]{1,0:T(8,128)(2,1)S(1)}, u32[]{:S(2)}, u32[]{:S(2)}) collective-permute-start(bf16[64,2048]{1,0:T(8,128)(2,1)S(1)} %get-tuple-element.11.refs_0_), channel_id=1, source_target_pairs={{0,16},{8,24},{16,0},{24,8},{1,17},{9,25},{17,1},{25,9},{2,18},{10... | collective-permute-start | bytes 786440 | tf_op jit(solution)/shard_map/ppermute | solution.py:427
  17.3 8.3 %collective-permute-start = (bf16[64,2048]{1,0:T(8,128)(2,1)S(1)}, bf16[64,2048]{1,0:T(8,128)(2,1)S(1)}, u32[]{:S(2)}, u32[]{:S(2)}) collective-permute-start(bf16[64,2048]{1,0:T(8,128)(2,1)S(1)} %get-tuple-element.11.refs_0_), channel_id=1, source_target_pairs={{0,8},{8,0},{16,24},{24,16},{1,9},{9,1},{17,25},{25,17},{2,10},{10... | collective-permute-start | bytes 786440 | tf_op jit(solution)/shard_map/ppermute | solution.py:427
  17.3 8.5 %copy-start.1 = (s32[16,30]{1,0:T(8,128)S(1)}, s32[16,30]{1,0:T(8,128)}, u32[]{:S(2)}) copy-start(s32[16,30]{1,0:T(8,128)} %occupancy_ref.3) | copy-start | bytes 5764
  24.1 1.7 %collective-permute-start.2 = (bf16[64,2048]{1,0:T(8,128)(2,1)S(1)}, bf16[64,2048]{1,0:T(8,128)(2,1)S(1)}, u32[]{:S(2)}, u32[]{:S(2)}) collective-permute-start(bf16[64,2048]{1,0:T(8,128)(2,1)S(1)} %collective-permute-done.1.refs_2_), channel_id=1, source_target_pairs={{0,8},{8,0},{16,24},{24,16},{1,9},{9,1},{17,25},{25,17},{2,10},{10... | collective-permute-start | bytes 786440 | tf_op jit(solution)/shard_map/ppermute | solution.py:427
  24.6 7.9 %collective-permute-start.4 = (bf16[64,1920]{1,0:T(8,128)(2,1)S(1)}, bf16[64,1920]{1,0:T(8,128)(2,1)S(1)}, u32[]{:S(2)}, u32[]{:S(2)}) collective-permute-start(bf16[64,1920]{1,0:T(8,128)(2,1)S(1)} %expand_last.1.refs_0_), channel_id=1, source_target_pairs={{0,16},{8,24},{16,0},{24,8},{1,17},{9,25},{17,1},{25,9},{2,18},{10... | collective-permute-start | bytes 737288 | tf_op jit(solution)/shard_map/ppermute | solution.py:427
  25.4 7.4 %collective-permute-start.3 = (bf16[64,1920]{1,0:T(8,128)(2,1)S(1)}, bf16[64,1920]{1,0:T(8,128)(2,1)S(1)}, u32[]{:S(2)}, u32[]{:S(2)}) collective-permute-start(bf16[64,1920]{1,0:T(8,128)(2,1)S(1)} %expand_last.1.refs_0_), channel_id=1, source_target_pairs={{0,8},{8,0},{16,24},{24,16},{1,9},{9,1},{17,25},{25,17},{2,10},{10... | collective-permute-start | bytes 737288 | tf_op jit(solution)/shard_map/ppermute | solution.py:427
  32.6 1.5 %collective-permute-start.5 = (bf16[64,1920]{1,0:T(8,128)(2,1)S(1)}, bf16[64,1920]{1,0:T(8,128)(2,1)S(1)}, u32[]{:S(2)}, u32[]{:S(2)}) collective-permute-start(bf16[64,1920]{1,0:T(8,128)(2,1)S(1)} %collective-permute-done.4.refs_2_), channel_id=1, source_target_pairs={{0,8},{8,0},{16,24},{24,16},{1,9},{9,1},{17,25},{25,17},{2,10},{10... | collective-permute-start | bytes 737288 | tf_op jit(solution)/shard_map/ppermute | solution.py:427
  34.1 10.0 %copy-start = (s32[64,32]{0,1:T(8,128)S(1)}, s32[64,32]{0,1:T(8,128)}, u32[]{:S(2)}) copy-start(s32[64,32]{0,1:T(8,128)} %param.19) | copy-start | bytes 24580
  38.6 21.1 %all-to-all-start = ((bf16[32,64,128]{2,1,0:T(8,128)(2,1)}), bf16[32,64,128]{2,1,0:T(8,128)(2,1)S(1)}, u32[]{:S(2)}, u32[]{:S(2)}) async-start(bf16[32,64,128]{2,1,0:T(8,128)(2,1)} %bitcast.4), calls=%async_computation | async-start | bytes 1048576 | tf_op jit(solution)/shard_map/all_to_all | solution.py:508

commit v5 on v4

--- a/solution.py
+++ b/solution.py
@@ -103,8 +103,8 @@
         copies.append(copy)
         copy.start()
 
-    half = pl.ds(0, GROUP)
-    other = pl.ds(GROUP, queries - GROUP)
+    half = pl.ds(0, 2 * GROUP)
+    other = pl.ds(2 * GROUP, queries - 2 * GROUP)
     bring(tokens_hbm, tokens_ref)
     bring(bias_hbm, bias_ref.at[0])
     bring(gain_hbm, gain_ref.at[0])
@@ -137,6 +137,7 @@
     def _():
         place_of(rows, live_at, tokens_ref)
         normed(0)
+        normed(1)
 
     for copy in copies[early:middle]:
         copy.wait()
@@ -145,8 +146,8 @@
     @pl.when(always)
     def _():
         for group in range(groups):
-            if group + 1 < groups:
-                normed(group + 1)
+            if group + 2 < groups:
+                normed(group + 2)
             part = normed_ref[group * rows : (group + 1) * rows, :]
             pool(part, decoder_ref, decoder_bias_ref[:, :chunk], group, length, pooled)
         out_ref[:, :chunk] = keep_vocab(start_ref[0], pooled)

time: 61.8 us -> 61.4 us (level)
  transfers between devices with their start and end apart: 7 -> 7, of which waited for: 4 -> 4; matrix products, arithmetic and copies ran while one was open for 1% -> 1% of each run, Pallas kernels for 22% -> 23%
where the time goes in v5:
time: 61.4 us; the launch traced here: 61 us
  Pallas kernels  33.3 us (54%)
  waiting for transfers between devices  15.9 us (26%)
  starting transfers between devices  10.3 us (17%)
  other arithmetic  0.81 us (1%)
  between operations  0.71 us (1%)
    pallas_call x6, Pallas kernels, call(): pl.pallas_call(kernel, in_specs=in_specs, out_specs=jax.tree.map(lambda _...  33.3 us
    all_to_all x1, waiting for transfers between devices, body(): lax.all_to_all(sent.reshape(everyone, steps * share, LANES), ('term', 'do...  14.2 us
    all_to_all x1, starting transfers between devices, body(): lax.all_to_all(sent.reshape(everyone, steps * share, LANES), ('term', 'do...  5.54 us
    ppermute x6, starting transfers between devices, spread(): held[k | bit] = lax.ppermute(held[k], 'doc', xor[bit])  4.8 us
    ppermute x6, waiting for transfers between devices, spread(): held[k | bit] = lax.ppermute(held[k], 'doc', xor[bit])  1.65 us
  transfers between devices with their start and end apart: 7, of which 4 were waited for; matrix products, arithmetic and copies ran while one was open for 1% of the time, Pallas kernels for 23%

profile of v5, /device:TPU:0, one launch (start us, length us, event | category | flops | bytes accessed | tf_op | source)
XLA Modules:
  0.0 61.0 jit_solution(4235888841501955341)
XLA Ops:
  0.6 13.3 %expand_first.1 = (bf16[64,2048]{1,0:T(8,128)(2,1)S(1)}, bf16[2048,768]{1,0:T(8,128)(2,1)S(1)}, bf16[768,1920]{1,0:T(8,128)(2,1)S(1)}, f32[1,3840]{1,0:T(1,128)S(1)}) custom-call(s32[1]{0:T(128)} %bitcast.start_ref, bf16[64,32,768]{2,1,0:T(8,128)(2,1)} %states_hbm.1, s32[32,64]{1,0:T(8,128)} %bitcast.12, bf16[768,768]{1,0:T(8,128)(2,1)} %transform_hbm.1, ...), custom_call_target="tpu_custom_call" | custom-call | flops 8455716864 | bytes 1000000 | tf_op jit(solution)/shard_map/expand_first/pallas_call | solution.py:394
  13.9 3.0 %collective-permute-start.1 = (bf16[64,2048]{1,0:T(8,128)(2,1)S(1)}, bf16[64,2048]{1,0:T(8,128)(2,1)S(1)}, u32[]{:S(2)}, u32[]{:S(2)}) collective-permute-start(bf16[64,2048]{1,0:T(8,128)(2,1)S(1)} %get-tuple-element.11.refs_0_), channel_id=1, source_target_pairs={{0,16},{8,24},{16,0},{24,8},{1,17},{9,25},{17,1},{25,9},{2,18},{10... | collective-permute-start | bytes 786440 | tf_op jit(solution)/shard_map/ppermute | solution.py:428
  16.9 0.0 collective-permute-start
  16.9 0.0 copy-start.1
  16.9 6.7 %expand_last.1.refs_0_ = bf16[64,1920]{1,0:T(8,128)(2,1)S(1)} custom-call(s32[1]{0:T(128)} %bitcast.start_ref, bf16[2048,768]{1,0:T(8,128)(2,1)S(1)} %get-tuple-element.12.normed_ref, bf16[768,1920]{1,0:T(8,128)(2,1)S(1)} %get-tuple-element.13.decoder_ref, f32[1,3840]{1,0:T(1,128)S(1)} %get-tuple-element.14.decoder_bias_ref), custom_call_target="tpu_custom_call" | custom-call | flops 6039797760 | bytes 1000000 | tf_op jit(solution)/shard_map/expand_last/pallas_call | solution.py:394
  23.6 0.0 collective-permute-done.1.refs_2_
  23.7 0.6 collective-permute-start.2
  24.2 0.7 %collective-permute-start.4 = (bf16[64,1920]{1,0:T(8,128)(2,1)S(1)}, bf16[64,1920]{1,0:T(8,128)(2,1)S(1)}, u32[]{:S(2)}, u32[]{:S(2)}) collective-permute-start(bf16[64,1920]{1,0:T(8,128)(2,1)S(1)} %expand_last.1.refs_0_), channel_id=1, source_target_pairs={{0,16},{8,24},{16,0},{24,8},{1,17},{9,25},{17,1},{25,9},{2,18},{10... | collective-permute-start | bytes 737288 | tf_op jit(solution)/shard_map/ppermute | solution.py:428
  25.0 0.2 collective-permute-start.3
  25.2 0.0 collective-permute-done.refs_1_
  25.2 0.2 collective-permute-done.2.refs_3_
  25.4 0.0 copy-done.1
  25.4 6.6 %score_first.1 = (f32[2048,256]{1,0:T(8,128)S(1)}, bf16[16,15,128,128]{3,2,1,0:T(8,128)(2,1)S(1)}, s32[4,512]{1,0:T(4,128)S(1)}) custom-call(s32[1]{0:T(128)} %bitcast.3.place_ref, s32[16,30]{1,0:T(8,128)S(1)} %copy-done.1, bf16[16,30,128,128]{3,2,1,0:T(8,128)(2,1)} %far_ref.1, bf16[64,2048]{1,0:T(8,128)(2,1)S(1)} %get-tuple-element.11.refs_0_, ...), custom_call_target="tpu_custom_call" | custom-call | flops 8053063680 | bytes 1000000 | tf_op jit(solution)/shard_map/score_first/pallas_call | solution.py:394
  32.0 0.2 collective-permute-done.4.refs_2_
  32.2 0.2 collective-permute-start.5
  32.4 0.0 collective-permute-done.3.refs_1_
  32.4 1.3 %collective-permute-done.5.refs_3_ = bf16[64,1920]{1,0:T(8,128)(2,1)S(1)} collective-permute-done((bf16[64,1920]{1,0:T(8,128)(2,1)S(1)}, bf16[64,1920]{1,0:T(8,128)(2,1)S(1)}, u32[]{:S(2)}, u32[]{:S(2)}) %collective-permute-start.5) | collective-permute-done | bytes 245792 | tf_op jit(solution)/shard_map/ppermute | solution.py:428
  33.7 0.0 copy-start
  33.7 4.4 %score_last.1 = bf16[8,4,64,128]{3,2,1,0:T(8,128)(2,1)} custom-call(s32[1]{0:T(128)} %bitcast.3.place_ref, s32[16,30]{1,0:T(8,128)S(1)} %copy-done.1, bf16[16,15,128,128]{3,2,1,0:T(8,128)(2,1)S(1)} %get-tuple-element.16.docs_ref, f32[2048,256]{1,0:T(8,128)S(1)} %get-tuple-element.17.before_ref, s32[4,512]{1,0:T(4,128)S(1)} %get-tuple-element.18.slots_ref, ...), custom_call_target="tpu_custom_call" | custom-call | flops 8053063680 | bytes 1000000 | tf_op jit(solution)/shard_map/score_last/pallas_call | solution.py:394
  38.1 5.5 %all-to-all-start = ((bf16[32,64,128]{2,1,0:T(8,128)(2,1)}), bf16[32,64,128]{2,1,0:T(8,128)(2,1)S(1)}, u32[]{:S(2)}, u32[]{:S(2)}) async-start(bf16[32,64,128]{2,1,0:T(8,128)(2,1)} %bitcast.4), calls=%async_computation | async-start | bytes 1048576 | tf_op jit(solution)/shard_map/all_to_all | solution.py:509
  43.7 0.0 copy-done
  43.7 0.5 choices.1.choice_ref
  44.2 0.8 %pad_maximum_fusion = bf16[64,3840]{1,0:T(8,128)(2,1)} fusion(bf16[64,1920]{1,0:T(8,128)(2,1)S(1)} %expand_last.1.refs_0_, bf16[64,1920]{1,0:T(8,128)(2,1)S(1)} %slice.3), kind=kLoop, calls=%fused_computation | loop fusion | flops 983040 | bytes 983040 | tf_op jit(solution)/shard_map/concatenate | solution.py:506
  45.0 14.2 %all-to-all-done = bf16[32,64,128]{2,1,0:T(8,128)(2,1)S(1)} async-done(((bf16[32,64,128]{2,1,0:T(8,128)(2,1)}), bf16[32,64,128]{2,1,0:T(8,128)(2,1)S(1)}, u32[]{:S(2)}, u32[]{:S(2)}) %all-to-all-start) | async-done | bytes 524320 | tf_op jit(solution)/shard_map/all_to_all | solution.py:509
  59.2 1.8 %place.1 = f32[32,16,64]{2,1,0:T(8,128)} custom-call(s32[32,64]{1,0:T(8,128)S(1)} %bitcast.10, bf16[16,128,256]{2,1,0:T(8,128)(2,1)S(1)} %choices.1.choice_ref, bf16[8,4,64,128]{3,2,1,0:T(8,128)(2,1)S(1)} %bitcast.7), custom_call_target="tpu_custom_call" | custom-call | flops 2000000 | bytes 1000000 | tf_op jit(solution)/shard_map/place/pallas_call | solution.py:394
  (1 shorter events, 0.0 us)
Async XLA Ops:
  13.9 9.7 %collective-permute-start.1 = (bf16[64,2048]{1,0:T(8,128)(2,1)S(1)}, bf16[64,2048]{1,0:T(8,128)(2,1)S(1)}, u32[]{:S(2)}, u32[]{:S(2)}) collective-permute-start(bf16[64,2048]{1,0:T(8,128)(2,1)S(1)} %get-tuple-element.11.refs_0_), channel_id=1, source_target_pairs={{0,16},{8,24},{16,0},{24,8},{1,17},{9,25},{17,1},{25,9},{2,18},{10... | collective-permute-start | bytes 786440 | tf_op jit(solution)/shard_map/ppermute | solution.py:428
  16.9 8.3 %collective-permute-start = (bf16[64,2048]{1,0:T(8,128)(2,1)S(1)}, bf16[64,2048]{1,0:T(8,128)(2,1)S(1)}, u32[]{:S(2)}, u32[]{:S(2)}) collective-permute-start(bf16[64,2048]{1,0:T(8,128)(2,1)S(1)} %get-tuple-element.11.refs_0_), channel_id=1, source_target_pairs={{0,8},{8,0},{16,24},{24,16},{1,9},{9,1},{17,25},{25,17},{2,10},{10... | collective-permute-start | bytes 786440 | tf_op jit(solution)/shard_map/ppermute | solution.py:428
  16.9 8.5 %copy-start.1 = (s32[16,30]{1,0:T(8,128)S(1)}, s32[16,30]{1,0:T(8,128)}, u32[]{:S(2)}) copy-start(s32[16,30]{1,0:T(8,128)} %occupancy_ref.3) | copy-start | bytes 5764
  23.7 1.7 %collective-permute-start.2 = (bf16[64,2048]{1,0:T(8,128)(2,1)S(1)}, bf16[64,2048]{1,0:T(8,128)(2,1)S(1)}, u32[]{:S(2)}, u32[]{:S(2)}) collective-permute-start(bf16[64,2048]{1,0:T(8,128)(2,1)S(1)} %collective-permute-done.1.refs_2_), channel_id=1, source_target_pairs={{0,8},{8,0},{16,24},{24,16},{1,9},{9,1},{17,25},{25,17},{2,10},{10... | collective-permute-start | bytes 786440 | tf_op jit(solution)/shard_map/ppermute | solution.py:428
  24.2 7.9 %collective-permute-start.4 = (bf16[64,1920]{1,0:T(8,128)(2,1)S(1)}, bf16[64,1920]{1,0:T(8,128)(2,1)S(1)}, u32[]{:S(2)}, u32[]{:S(2)}) collective-permute-start(bf16[64,1920]{1,0:T(8,128)(2,1)S(1)} %expand_last.1.refs_0_), channel_id=1, source_target_pairs={{0,16},{8,24},{16,0},{24,8},{1,17},{9,25},{17,1},{25,9},{2,18},{10... | collective-permute-start | bytes 737288 | tf_op jit(solution)/shard_map/ppermute | solution.py:428
  25.0 7.4 %collective-permute-start.3 = (bf16[64,1920]{1,0:T(8,128)(2,1)S(1)}, bf16[64,1920]{1,0:T(8,128)(2,1)S(1)}, u32[]{:S(2)}, u32[]{:S(2)}) collective-permute-start(bf16[64,1920]{1,0:T(8,128)(2,1)S(1)} %expand_last.1.refs_0_), channel_id=1, source_target_pairs={{0,8},{8,0},{16,24},{24,16},{1,9},{9,1},{17,25},{25,17},{2,10},{10... | collective-permute-start | bytes 737288 | tf_op jit(solution)/shard_map/ppermute | solution.py:428
  32.2 1.5 %collective-permute-start.5 = (bf16[64,1920]{1,0:T(8,128)(2,1)S(1)}, bf16[64,1920]{1,0:T(8,128)(2,1)S(1)}, u32[]{:S(2)}, u32[]{:S(2)}) collective-permute-start(bf16[64,1920]{1,0:T(8,128)(2,1)S(1)} %collective-permute-done.4.refs_2_), channel_id=1, source_target_pairs={{0,8},{8,0},{16,24},{24,16},{1,9},{9,1},{17,25},{25,17},{2,10},{10... | collective-permute-start | bytes 737288 | tf_op jit(solution)/shard_map/ppermute | solution.py:428
  33.7 10.0 %copy-start = (s32[64,32]{0,1:T(8,128)S(1)}, s32[64,32]{0,1:T(8,128)}, u32[]{:S(2)}) copy-start(s32[64,32]{0,1:T(8,128)} %param.19) | copy-start | bytes 24580
  38.1 21.1 %all-to-all-start = ((bf16[32,64,128]{2,1,0:T(8,128)(2,1)}), bf16[32,64,128]{2,1,0:T(8,128)(2,1)S(1)}, u32[]{:S(2)}, u32[]{:S(2)}) async-start(bf16[32,64,128]{2,1,0:T(8,128)(2,1)} %bitcast.4), calls=%async_computation | async-start | bytes 1048576 | tf_op jit(solution)/shard_map/all_to_all | solution.py:509
